TPU v7x, 512 devices: a whole 4x4x16 slice. The times are simulated.
512 devices in a mesh: space: 64 (over x, z_hi, y, core), vec: 8 (over z_lo).
Axes of the slice: x: 4, y: 4, z: 16 (z_hi: 2, z_lo: 8; z = z_hi * 8 + z_lo), core: 2. Of those that a mesh axis runs over, the one named last changes fastest.
Arguments:
- vectors: bfloat16 [64, 3, 2, 256, 1024], P('space', None, None, 'vec'), may hold values from -6 to 6
- links: float32 [64, 3, 3, 3, 2, 1024], P('space'), may hold values from -2.5 to 2.5
- directions: int32 [3], replicated, may hold values from 0 to 2, each once
- offsets: int32 [5], replicated, may hold values from 0 to 4, each once
Outputs:
- elementals: float32 [3, 5, 2, 8, 1024], P(None, None, None, 'vec', 'space')
Inputs may be any that keep to these rules, and one draw needn't show every extreme that they name: Each of the three lattice directions appears once. `offsets`: each block offset 0 to 4 appears once.
All inputs are finite; a program needn't handle non-finite values.
Results may differ from a plain program's by a relative error of at most 0.0029.
Values may be sent and summed in bfloat16 or wider, within the bound.
A program may use at most 64 MiB of HBM per device.

v0:
```python
import math

import jax
import jax.numpy as jnp
from jax import lax
from jax.sharding import PartitionSpec as P

LY = 64
LZ = 16


def passed_along(shard, axis, by):
    devices = lax.axis_size(axis)
    return lax.ppermute(shard, axis, [(i, (i + by) % devices) for i in range(devices)])


def with_halo(shard, sides, width):
    for axis, dim in sides:
        devices, length = (lax.axis_size(axis), shard.shape[dim])
        up = [(i, (i + 1) % devices) for i in range(devices)]
        down = [(j, i) for i, j in up]
        last = lax.slice_in_dim(shard, length - width, length, axis=dim)
        initial = lax.slice_in_dim(shard, 0, width, axis=dim)
        before = lax.ppermute(last, axis, up)
        after = lax.ppermute(initial, axis, down)
        shard = jnp.concatenate([before, shard, after], axis=dim)
    return shard


def apply_link(link, vec):
    terms_re = []
    terms_im = []
    for col in range(3):
        link_re = link[:, col, 0][:, None, :]
        link_im = link[:, col, 1][:, None, :]
        vec_re = vec[col, 0][None]
        vec_im = vec[col, 1][None]
        terms_re.append(link_re * vec_re - link_im * vec_im)
        terms_im.append(link_re * vec_im + link_im * vec_re)
    real_part = terms_re[0] + terms_re[1] + terms_re[2]
    imag_part = terms_im[0] + terms_im[1] + terms_im[2]
    return jnp.stack([real_part, imag_part], axis=1)


def apply_dagger(link, vec):
    terms_re = []
    terms_im = []
    for col in range(3):
        link_re = link[col, :, 0][:, None, :]
        link_im = link[col, :, 1][:, None, :]
        vec_re = vec[col, 0][None]
        vec_im = vec[col, 1][None]
        terms_re.append(link_re * vec_re + link_im * vec_im)
        terms_im.append(link_re * vec_im - link_im * vec_re)
    real_part = terms_re[0] + terms_re[1] + terms_re[2]
    imag_part = terms_im[0] + terms_im[1] + terms_im[2]
    return jnp.stack([real_part, imag_part], axis=1)


def shift_plane(field, axis_mu, step):
    if axis_mu == 1:
        return jnp.roll(field, -step * LZ, axis=-1)
    shaped = field.reshape(field.shape[:-1] + (LY, LZ))
    return jnp.roll(shaped, -step, axis=-1).reshape(field.shape)


def body(vectors, links, directions, offsets):
    own = vectors[0]
    block_width = own.shape[2]
    count_off = offsets.shape[0]
    planes_total = lax.axis_size("space") * vectors.shape[0]
    scale = 1.0 / math.sqrt(6.0 * planes_total * LY * LZ)
    plane_links = links[0]
    lower_x = passed_along(links[:, 0], "space", 1)[0]
    links_back = [None, shift_plane(plane_links[1], 1, -1), shift_plane(plane_links[2], 2, -1)]
    padded = with_halo(own[None], (("space", 0),), 1)
    below = padded[0].astype(jnp.float32)
    centre = padded[1].astype(jnp.float32)
    above = padded[2].astype(jnp.float32)
    results = [apply_link(plane_links[0], above) + apply_dagger(lower_x, below)]
    for axis_mu in (1, 2):
        forward = apply_link(plane_links[axis_mu], shift_plane(centre, axis_mu, 1))
        backward = apply_dagger(links_back[axis_mu], shift_plane(centre, axis_mu, -1))
        results.append(forward + backward)
    displaced = jnp.stack(results).astype(jnp.bfloat16)
    swapped = jnp.stack([-displaced[:, :, 1], displaced[:, :, 0]], axis=2)
    stacked = jnp.stack([displaced, swapped], axis=1)
    terms = []
    travel = own
    for step in range(count_off):
        if step > 0:
            travel = passed_along(travel, "vec", 1)
        terms.append(
            jnp.einsum("mtcprs,cpqs->mtrq", stacked, travel, preferred_element_type=jnp.float32)
            * scale
        )
    blocks = jnp.stack(terms)
    dir_table = (directions[:, None] == jnp.arange(3, dtype=jnp.int32)[None, :]).astype(jnp.float32)
    off_table = (offsets[:, None] == jnp.arange(count_off, dtype=jnp.int32)[None, :]).astype(
        jnp.float32
    )
    chosen = jnp.einsum(
        "dm,jk,kmprc->djprc", dir_table, off_table, blocks, precision=lax.Precision.HIGHEST
    )
    partial_value = chosen.reshape(3, count_off, 2, 1, block_width * block_width)
    total = lax.psum(partial_value, "space")
    share = block_width * block_width // lax.axis_size("space")
    return lax.dynamic_slice_in_dim(total, lax.axis_index("space") * share, share, 4)


def solution(mesh):
    placed = (
        P("space", None, None, "vec", None),
        P("space", None, None, None, None, None),
        P(),
        P(),
    )
    return jax.shard_map(
        body,
        mesh=mesh,
        in_specs=placed,
        out_specs=P(None, None, None, "vec", "space"),
        check_vma=False,
    )
```

profile of v0, /device:TPU:1, one launch (start us, length us, event | category | flops | bytes accessed | tf_op | source)
XLA Modules:
  0.0 1152.5 jit_solution(382275088152394286)
XLA Ops:
  6.5 8.8 collective-permute-start
  15.3 1.9 collective-permute-start.2
  17.3 1.7 slice_bitcast_fusion.25
  19.0 1.9 collective-permute-start.1
  20.9 1.9 collective-permute-start.3
  22.8 1.5 copy.63
  25.7 1.5 fusion.62
  27.9 1.1 pad_maximum_fusion
  29.0 1.7 slice_bitcast_fusion.11
  30.7 1.2 copy.69
  32.6 1.9 copy.68
  34.5 1.9 copy.67
  36.3 1.9 copy.66
  38.2 1.9 copy.65
  40.1 1.9 copy.64
  42.0 1.7 slice_bitcast_fusion.5
  43.7 1.9 copy.76
  46.3 1.0 reshape.763
  47.3 1.6 fusion.66
  48.8 1.2 copy.75
  59.6 1.1 bitcast_convert_fusion.1
  60.7 1.1 bitcast_convert_fusion
  62.8 2.1 collective-permute-start.4
  65.1 13.2 %collective-permute-done.4 = bf16[3,2,32,1024]{3,2,1,0:T(8,128)(2,1)S(1)} collective-permute-done((bf16[3,2,32,1024]{3,2,1,0:T(8,128)(2,1)}, bf16[3,2,32,1024]{3,2,1,0:T(8,128)(2,1)S(1)}, u32[]{:S(2)}, u32[]{:S(2)}) %collective-permute-start.4) | collective-permute-done | bytes 393248 | tf_op jit(solution)/shard_map/ppermute | solution.py:14
  78.3 1.9 collective-permute-start.5
  81.0 1.8 fusion.11
  82.7 13.8 %collective-permute-done.5 = bf16[3,2,32,1024]{3,2,1,0:T(8,128)(2,1)S(1)} collective-permute-done((bf16[3,2,32,1024]{3,2,1,0:T(8,128)(2,1)S(1)}, bf16[3,2,32,1024]{3,2,1,0:T(8,128)(2,1)S(1)}, u32[]{:S(2)}, u32[]{:S(2)}) %collective-permute-start.5) | collective-permute-done | bytes 393248 | tf_op jit(solution)/shard_map/ppermute | solution.py:14
  96.5 2.1 collective-permute-start.6
  100.2 15.9 %collective-permute-done.6 = bf16[3,2,32,1024]{3,2,1,0:T(8,128)(2,1)S(1)} collective-permute-done((bf16[3,2,32,1024]{3,2,1,0:T(8,128)(2,1)S(1)}, bf16[3,2,32,1024]{3,2,1,0:T(8,128)(2,1)S(1)}, u32[]{:S(2)}, u32[]{:S(2)}) %collective-permute-start.6) | collective-permute-done | bytes 393248 | tf_op jit(solution)/shard_map/ppermute | solution.py:14
  116.9 0.9 fusion.19
  119.7 1024.5 %all-reduce.2.cloned.1.call-done = f32[3,5,2,1,1024]{4,2,1,0,3:T(2,128)} async-done(((f32[3,5,2,1,1024]{4,2,1,0,3:T(2,128)}), f32[3,5,2,1,1024]{4,2,1,0,3:T(2,128)}) %all-reduce.2.cloned.1.call-update) | async-done | bytes 122896 | tf_op jit(solution)/shard_map/psum | solution.py:106
  1144.2 1.4 constant_dynamic-slice_fusion
  (110 shorter events, 18.7 us)
Async XLA Ops:
  6.5 1137.7 %all-reduce.2.cloned.1.call-start = ((), (), s32[]{:S(2)}) async-start(), calls=%async_computation | async-start | bytes 245760 | tf_op jit(solution)/shard_map/psum | solution.py:106
  6.5 53.0 %collective-permute-start = (bf16[1,3,2,32,1024]{4,3,2,1,0:T(8,128)(2,1)}, bf16[1,3,2,32,1024]{4,3,2,1,0:T(8,128)(2,1)}, u32[]{:S(2)}, u32[]{:S(2)}) collective-permute-start(bf16[1,3,2,32,1024]{4,3,2,1,0:T(8,128)(2,1)} %param.4), channel_id=1, source_target_pairs={{8,0},{16,8},{24,16},{32,24},{40,32},{48,40},{56,48},{64,56},{72,6... | collective-permute-start | bytes 1179656 | tf_op jit(solution)/shard_map/ppermute | solution.py:25
  15.3 45.4 %collective-permute-start.2 = (bf16[1,3,2,32,1024]{4,3,2,1,0:T(8,128)(2,1)}, bf16[1,3,2,32,1024]{4,3,2,1,0:T(8,128)(2,1)}, u32[]{:S(2)}, u32[]{:S(2)}) collective-permute-start(bf16[1,3,2,32,1024]{4,3,2,1,0:T(8,128)(2,1)} %param.4), channel_id=1, source_target_pairs={{0,8},{8,16},{16,24},{24,32},{32,40},{40,48},{48,56},{56,64},{64,7... | collective-permute-start | bytes 1179656 | tf_op jit(solution)/shard_map/ppermute | solution.py:24
  19.0 39.6 %collective-permute-start.1 = (f32[1,3,3,2,1024]{4,3,2,1,0:T(2,128)}, f32[1,3,3,2,1024]{4,3,2,1,0:T(2,128)}, u32[]{:S(2)}, u32[]{:S(2)}) collective-permute-start(f32[1,3,3,2,1024]{4,3,2,1,0:T(2,128)} %get-tuple-element.63), channel_id=1, source_target_pairs={{0,8},{8,16},{16,24},{24,32},{32,40},{40,48},{48,56},{56,64},{64,7... | collective-permute-start | bytes 221192 | tf_op jit(solution)/shard_map/ppermute | solution.py:14
  20.9 41.9 %collective-permute-start.3 = (bf16[3,2,32,1024]{3,2,1,0:T(8,128)(2,1)}, bf16[3,2,32,1024]{3,2,1,0:T(8,128)(2,1)}, u32[]{:S(2)}, u32[]{:S(2)}) collective-permute-start(bf16[3,2,32,1024]{3,2,1,0:T(8,128)(2,1)} %bitcast.340), channel_id=1, source_target_pairs={{0,1},{1,2},{2,3},{3,4},{4,5},{5,6},{6,7},{7,0},{8,9},{9,10},{10,1... | collective-permute-start | bytes 1179656 | tf_op jit(solution)/shard_map/ppermute | solution.py:14
  24.7 1.0 copy-start.6
  42.0 3.6 copy-start.16
  45.8 4.2 copy-start.5
  45.8 4.4 copy-start.4
  46.0 4.4 copy-start.3
  46.0 4.5 copy-start.2
  46.3 8.9 copy-start.8
  46.3 8.9 copy-start.9
  46.3 8.9 copy-start.10
  46.3 8.9 copy-start.11
  47.3 8.0 copy-start.13
  50.0 5.5 copy-start.12
  55.8 1.1 copy-start.1
  55.8 1.1 copy-start.15
  56.0 1.3 copy-start
  56.0 1.3 copy-start.14
  62.8 17.4 %copy-start.7 = (bf16[1,3,2,32,1024]{4,3,2,1,0:T(8,128)(2,1)S(1)}, bf16[1,3,2,32,1024]{4,3,2,1,0:T(8,128)(2,1)}, u32[]{:S(2)}) copy-start(bf16[1,3,2,32,1024]{4,3,2,1,0:T(8,128)(2,1)} %param.4) | copy-start | bytes 1179652
  62.8 15.5 %collective-permute-start.4 = (bf16[3,2,32,1024]{3,2,1,0:T(8,128)(2,1)}, bf16[3,2,32,1024]{3,2,1,0:T(8,128)(2,1)S(1)}, u32[]{:S(2)}, u32[]{:S(2)}) collective-permute-start(bf16[3,2,32,1024]{3,2,1,0:T(8,128)(2,1)} %collective-permute-done.3), channel_id=1, source_target_pairs={{0,1},{1,2},{2,3},{3,4},{4,5},{5,6},{6,7},{7,0},{8,9},{9,10},{10,1... | collective-permute-start | bytes 1179656 | tf_op jit(solution)/shard_map/ppermute | solution.py:14
  78.3 18.2 %collective-permute-start.5 = (bf16[3,2,32,1024]{3,2,1,0:T(8,128)(2,1)S(1)}, bf16[3,2,32,1024]{3,2,1,0:T(8,128)(2,1)S(1)}, u32[]{:S(2)}, u32[]{:S(2)}) collective-permute-start(bf16[3,2,32,1024]{3,2,1,0:T(8,128)(2,1)S(1)} %collective-permute-done.4), channel_id=1, source_target_pairs={{0,1},{1,2},{2,3},{3,4},{4,5},{5,6},{6,7},{7,0},{8,9},{9,10},{10,1... | collective-permute-start | bytes 1179656 | tf_op jit(solution)/shard_map/ppermute | solution.py:14
  96.5 19.6 %collective-permute-start.6 = (bf16[3,2,32,1024]{3,2,1,0:T(8,128)(2,1)S(1)}, bf16[3,2,32,1024]{3,2,1,0:T(8,128)(2,1)S(1)}, u32[]{:S(2)}, u32[]{:S(2)}) collective-permute-start(bf16[3,2,32,1024]{3,2,1,0:T(8,128)(2,1)S(1)} %collective-permute-done.5), channel_id=1, source_target_pairs={{0,1},{1,2},{2,3},{3,4},{4,5},{5,6},{6,7},{7,0},{8,9},{9,10},{10,1... | collective-permute-start | bytes 1179656 | tf_op jit(solution)/shard_map/ppermute | solution.py:14
  100.1 16.8 %copy-start.17 = (s32[3]{0:T(128)S(1)}, s32[3]{0:T(128)}, u32[]{:S(2)}) copy-start(s32[3]{0:T(128)} %param.6) | copy-start | bytes 40
  100.2 17.7 %copy-start.18 = (s32[5]{0:T(128)S(1)}, s32[5]{0:T(128)}, u32[]{:S(2)}) copy-start(s32[5]{0:T(128)} %param.7) | copy-start | bytes 64
Sparse Core Ops, SparseCore 0:
  119.8 1024.3 all-reduce.1
where the time goes:
time: 1160 us; the launch traced here: 1150 us
  waiting for transfers between devices  1070 us (92%)
  local copies, waits for them, and re-layouts  37 us (3%)
  starting transfers between devices  20.6 us (2%)
  between operations  14.1 us (1%)
    psum x1, waiting for transfers between devices, body(): total = lax.psum(partial_value, 'space')  1020 us
    ppermute x5, waiting for transfers between devices, passed_along(): lax.ppermute(shard, axis, [(i, (i + by) % devices) for i in range(devices)])  42.9 us
  transfers between devices with their start and end apart: 8, of which 4 were waited for; matrix products, arithmetic and copies ran while one was open for 4% of the time, Pallas kernels for 0%

commit v1 on v0

v1 whole, which is shorter than its diff:
```python
import functools
import math

import jax
import jax.numpy as jnp
from jax import lax
from jax.experimental import pallas as pl
from jax.experimental.pallas import tpu as pltpu
from jax.sharding import PartitionSpec as P

LY = 64
LZ = 16
SITES = LY * LZ
VB = 32
HOPS = 4
NX, NH, NY, NC = 4, 2, 4, 2
CHIPS = NX * NH * NY


def send(src, dst, send_sem, recv_sem, **where):
    return pltpu.make_async_remote_copy(
        src_ref=src,
        dst_ref=dst,
        send_sem=send_sem,
        recv_sem=recv_sem,
        device_id=where,
        device_id_type=pl.DeviceIdType.MESH,
    )


def displace(rows, above, below, forward, backward, shifted):
    row0 = rows * 2 * VB

    def step(at, carry):
        half = lax.rem(at, 2)
        first = pl.multiple_of(half * 16, 16)
        lanes = pl.ds(pl.multiple_of(lax.div(at, 2) * 128, 128), 128)
        up = [[above[c, p, pl.ds(first, 16), lanes].astype(jnp.float32) for p in range(2)] for c in range(3)]
        down = [[below[c, p, pl.ds(first, 16), lanes].astype(jnp.float32) for p in range(2)] for c in range(3)]
        for row in range(3):
            terms_re = []
            terms_im = []
            back_re = []
            back_im = []
            for col in range(3):
                link_re = forward[row, col, pl.ds(0, 1), lanes]
                link_im = forward[row, col, pl.ds(1, 1), lanes]
                vec_re, vec_im = up[col]
                terms_re.append(link_re * vec_re - link_im * vec_im)
                terms_im.append(link_re * vec_im + link_im * vec_re)
                link_re = backward[col, row, pl.ds(0, 1), lanes]
                link_im = backward[col, row, pl.ds(1, 1), lanes]
                vec_re, vec_im = down[col]
                back_re.append(link_re * vec_re + link_im * vec_im)
                back_im.append(link_re * vec_im - link_im * vec_re)
            real = (terms_re[0] + terms_re[1] + terms_re[2]) + (back_re[0] + back_re[1] + back_re[2])
            imag = (terms_im[0] + terms_im[1] + terms_im[2]) + (back_im[0] + back_im[1] + back_im[2])
            shifted[row, pl.ds(row0 + first, 16), lanes] = real.astype(jnp.bfloat16)
            shifted[row, pl.ds(row0 + VB + first, 16), lanes] = imag.astype(jnp.bfloat16)
        return carry

    lax.fori_loop(0, 2 * SITES // 128, step, 0)


def z_moved(field, step):
    lane = lax.broadcasted_iota(jnp.int32, field.shape, field.ndim - 1)
    place = jnp.bitwise_and(lane, LZ - 1)
    last = field.ndim - 1
    if step == 1:
        return jnp.where(place == LZ - 1, pltpu.roll(field, LZ - 1, last), pltpu.roll(field, SITES - 1, last))
    return jnp.where(place == 0, pltpu.roll(field, SITES - LZ + 1, last), pltpu.roll(field, 1, last))


def kernel(
    vec_hbm,
    link_hbm,
    directions,
    offsets,
    out,
    blocks,
    above,
    below,
    links,
    lower,
    back,
    moved,
    shifted,
    acc,
    tiles,
    got_y,
    sum_y,
    got_x,
    sum_x,
    got_z,
    sum_z,
    got_c,
    picked,
    local_sem,
    ring_send,
    ring_recv,
    halo_send,
    halo_recv,
    y_send,
    y_recv,
    x_send,
    x_recv,
    pair_send,
    pair_recv,
    *,
    scale,
):
    space = lax.axis_index("space")
    vec = lax.axis_index("vec")
    planes = lax.axis_size("space")
    nvec = lax.axis_size("vec")
    core = lax.rem(space, NC)
    chip = lax.div(space, NC)
    y = lax.rem(chip, NY)
    z_hi = lax.rem(lax.div(chip, NY), NH)
    x = lax.div(chip, NY * NH)

    def at(x, z_hi, y, core):
        return ((x * NH + z_hi) * NY + y) * NC + core

    up = lax.rem(space + 1, planes)
    down = lax.rem(space + planes - 1, planes)
    after = lax.rem(vec + 1, nvec)
    before = lax.rem(vec + nvec - 1, nvec)
    y_peers = [at(x, z_hi, lax.rem(y + i, NY), core) for i in range(1, NY)]
    x_peers = [at(lax.rem(x + i, NX), z_hi, y, core) for i in range(1, NX)]
    z_peer = at(x, 1 - z_hi, y, core)
    c_peer = at(x, z_hi, y, 1 - core)

    own = pltpu.make_async_copy(vec_hbm.at[0], blocks.at[0], local_sem.at[0])
    own.start()
    links_in = pltpu.make_async_copy(link_hbm.at[0], links, local_sem.at[1])
    links_in.start()

    barrier = pltpu.get_barrier_semaphore()
    peers = [up, down, z_peer] + y_peers + x_peers
    for peer in peers:
        pl.semaphore_signal(barrier, inc=1, device_id={"space": peer}, device_id_type=pl.DeviceIdType.MESH)
    for peer in (after, before):
        pl.semaphore_signal(barrier, inc=1, device_id={"vec": peer}, device_id_type=pl.DeviceIdType.MESH)
    pl.semaphore_wait(barrier, len(peers) + 2)

    def hop(k, c):
        return send(blocks.at[k, c], blocks.at[k + 1, c], ring_send.at[k, c], ring_recv.at[k, c], vec=after)

    firsts = [
        send(vec_hbm.at[0, c], blocks.at[1, c], ring_send.at[0, c], ring_recv.at[0, c], vec=after) for c in range(3)
    ]
    for copy in firsts:
        copy.start()
    to_up = send(vec_hbm.at[0], below, halo_send.at[0], halo_recv.at[0], space=up)
    to_down = send(vec_hbm.at[0], above, halo_send.at[1], halo_recv.at[1], space=down)
    link_up = send(link_hbm.at[0, 0], lower, halo_send.at[2], halo_recv.at[2], space=up)
    to_up.start()
    to_down.start()
    link_up.start()

    own.wait()

    def move(i, carry):
        c = lax.div(i, 4)
        p = lax.rem(lax.div(i, 2), 2)
        rows = pl.ds(pl.multiple_of(lax.rem(i, 2) * 16, 16), 16)
        field = blocks[0, c, p, rows, :].astype(jnp.float32)
        moved[0, c, p, rows, :] = pltpu.roll(field, SITES - LZ, 1).astype(jnp.bfloat16)
        moved[1, c, p, rows, :] = pltpu.roll(field, LZ, 1).astype(jnp.bfloat16)
        moved[2, c, p, rows, :] = z_moved(field, 1).astype(jnp.bfloat16)
        moved[3, c, p, rows, :] = z_moved(field, -1).astype(jnp.bfloat16)
        return carry

    lax.fori_loop(0, 12, move, 0)
    links_in.wait()
    for row in range(3):
        for col in range(3):
            back[0, row, col] = pltpu.roll(links[1, row, col], LZ, 1)
            back[1, row, col] = z_moved(links[2, row, col], -1)
    displace(1, moved.at[0], moved.at[1], links.at[1], back.at[0], shifted)
    displace(2, moved.at[2], moved.at[3], links.at[2], back.at[1], shifted)

    def product(k, c, first, count):
        left = shifted[c, first : first + count, :]
        right = blocks[k, c].reshape(2 * VB, SITES)
        return lax.dot_general(left, right, (((1,), (1,)), ((), ())), preferred_element_type=jnp.float32)

    acc[...] = jnp.zeros_like(acc)
    yz = (2 * VB, 4 * VB)
    xs = (0, 2 * VB)

    def add(k, c, part):
        first, count = part
        acc[k, first : first + count, :] += product(k, c, first, count)

    def own_step(c, carry):
        add(0, c, yz)
        return carry

    lax.fori_loop(0, 3, own_step, 0)

    def ring_step(i, carry):
        k = lax.div(i, 3)
        c = lax.rem(i, 3)
        hop(k, c).wait_recv()
        hop(k + 1, c).start()
        add(k + 1, c, yz)
        return carry

    lax.fori_loop(0, 3 * (HOPS - 1), ring_step, 0)

    to_up.wait_recv()
    to_down.wait_recv()
    link_up.wait_recv()
    displace(0, above, below, links.at[0], lower, shifted)

    def x_step(i, carry):
        add(lax.div(i, 3), lax.rem(i, 3), xs)
        return carry

    lax.fori_loop(0, 3 * HOPS, x_step, 0)

    def last_step(c, carry):
        hop(HOPS - 1, c).wait_recv()
        add(HOPS, c, (0, 6 * VB))
        return carry

    lax.fori_loop(0, 3, last_step, 0)

    wide = [[] for _ in range(6)]
    tail = []
    for k in range(HOPS + 1):
        for mu in range(3):
            first = acc[k, mu * 2 * VB : mu * 2 * VB + VB, :]
            second = acc[k, mu * 2 * VB + VB : (mu + 1) * 2 * VB, :]
            real = first[:, :VB] + second[:, VB:]
            imag = first[:, VB:] - second[:, :VB]
            if k < HOPS:
                wide[2 * mu].append(real)
                wide[2 * mu + 1].append(imag)
            else:
                tail += [real, imag]
    for j in range(6):
        tiles[pl.ds(j, CHIPS, stride=8), :] = jnp.concatenate(wide[j], axis=1) * scale
    tiles[pl.ds(6, CHIPS, stride=8), :] = jnp.concatenate(tail[:4], axis=1) * scale
    empty = jnp.zeros((VB, 2 * VB), jnp.float32)
    tiles[pl.ds(7, CHIPS, stride=8), :] = jnp.concatenate(tail[4:] + [empty], axis=1) * scale

    sends = []

    def tile(xx, hh, yy):
        return pl.ds(pl.multiple_of(((xx * NH + hh) * NY + yy) * 8, 8), 8)

    for i in range(1, NY):
        yy = lax.rem(y + i, NY)
        for g in range(NX * NH):
            sends.append(
                send(
                    tiles.at[tile(0, g, yy)],
                    got_y.at[i - 1, pl.ds(g * 8, 8)],
                    y_send.at[i - 1, g],
                    y_recv.at[i - 1, g],
                    space=y_peers[i - 1],
                )
            )
            sends[-1].start()
    for copy in sends:
        copy.wait_recv()
    for g in range(NX * NH):
        total = tiles[tile(0, g, y), :]
        for i in range(NY - 1):
            total = total + got_y[i, pl.ds(g * 8, 8), :]
        sum_y[pl.ds(g * 8, 8), :] = total

    x_sends = []
    for i in range(1, NX):
        xx = lax.rem(x + i, NX)
        rows = pl.ds(pl.multiple_of(xx * NH * 8, 8), NH * 8)
        x_sends.append(
            send(sum_y.at[rows], got_x.at[i - 1], x_send.at[i - 1], x_recv.at[i - 1], space=x_peers[i - 1])
        )
        x_sends[-1].start()
    for copy in x_sends:
        copy.wait_recv()
    total = sum_y[pl.ds(pl.multiple_of(x * NH * 8, 8), NH * 8), :]
    for i in range(NX - 1):
        total = total + got_x[i]
    sum_x[...] = total

    z_copy = send(
        sum_x.at[pl.ds(pl.multiple_of((1 - z_hi) * 8, 8), 8)], got_z, pair_send.at[0], pair_recv.at[0], space=z_peer
    )
    z_copy.start()
    z_copy.wait_recv()
    sum_z[...] = sum_x[pl.ds(pl.multiple_of(z_hi * 8, 8), 8), :] + got_z[...]
    c_copy = send(sum_z, got_c, pair_send.at[1], pair_recv.at[1], space=c_peer)
    c_copy.start()
    c_copy.wait_recv()
    total = sum_z[...] + got_c[...]

    half = VB // 2
    for mu in range(3):
        for t in range(2):
            j = 2 * mu + t
            for k in range(HOPS + 1):
                row, lane = (j, k * VB) if k < HOPS else (6 + j // 4, (j % 4) * VB)
                low = total[row : row + 1, lane : lane + half]
                high = total[row : row + 1, lane + half : lane + VB]
                at_row = (mu * (HOPS + 1) + k) * 2 + t
                picked[at_row : at_row + 1, :half] = jnp.where(core == 0, low, high)
    for d in range(3):
        mu = directions[d]
        for q in range(HOPS + 1):
            rows = pl.ds((mu * (HOPS + 1) + offsets[q]) * 2, 2)
            out[d, q, :, 0, :] = picked[rows, :half]

    for copy in firsts + [to_up, to_down, link_up] + sends + x_sends + [z_copy, c_copy]:
        copy.wait_send()

    def drain(i, carry):
        hop(lax.div(i, 3) + 1, lax.rem(i, 3)).wait_send()
        return carry

    lax.fori_loop(0, 3 * (HOPS - 1), drain, 0)


def body(vectors, links, directions, offsets):
    planes = lax.axis_size("space")
    scale = 1.0 / math.sqrt(6.0 * planes * SITES)
    bf16, f32 = jnp.bfloat16, jnp.float32
    block = (3, 2, VB, SITES)
    dma = pltpu.SemaphoreType.DMA
    return pl.pallas_call(
        functools.partial(kernel, scale=scale),
        out_shape=jax.ShapeDtypeStruct((3, HOPS + 1, 2, 1, VB // 2), f32),
        in_specs=[
            pl.BlockSpec(memory_space=pl.ANY),
            pl.BlockSpec(memory_space=pl.ANY),
            pl.BlockSpec(memory_space=pltpu.SMEM),
            pl.BlockSpec(memory_space=pltpu.SMEM),
        ],
        out_specs=pl.BlockSpec(memory_space=pltpu.VMEM),
        scratch_shapes=[
            pltpu.VMEM((HOPS + 1,) + block, bf16),
            pltpu.VMEM(block, bf16),
            pltpu.VMEM(block, bf16),
            pltpu.VMEM((3, 3, 3, 2, SITES), f32),
            pltpu.VMEM((3, 3, 2, SITES), f32),
            pltpu.VMEM((2, 3, 3, 2, SITES), f32),
            pltpu.VMEM((4,) + block, bf16),
            pltpu.VMEM((3, 6 * VB, SITES), bf16),
            pltpu.VMEM((HOPS + 1, 6 * VB, 2 * VB), f32),
            pltpu.VMEM((CHIPS * 8, 128), f32),
            pltpu.VMEM((NY - 1, NX * NH * 8, 128), f32),
            pltpu.VMEM((NX * NH * 8, 128), f32),
            pltpu.VMEM((NX - 1, NH * 8, 128), f32),
            pltpu.VMEM((NH * 8, 128), f32),
            pltpu.VMEM((8, 128), f32),
            pltpu.VMEM((8, 128), f32),
            pltpu.VMEM((8, 128), f32),
            pltpu.VMEM((6 * (HOPS + 1) + 2, 128), f32),
            dma((2,)),
            dma((HOPS, 3)),
            dma((HOPS, 3)),
            dma((3,)),
            dma((3,)),
            dma((NY - 1, NX * NH)),
            dma((NY - 1, NX * NH)),
            dma((NX - 1,)),
            dma((NX - 1,)),
            dma((2,)),
            dma((2,)),
        ],
        compiler_params=pltpu.CompilerParams(
            collective_id=0, has_side_effects=True, vmem_limit_bytes=40 * 1024 * 1024
        ),
        name="elementals",
    )(vectors, links, directions, offsets)


def solution(mesh):
    placed = (
        P("space", None, None, "vec", None),
        P("space", None, None, None, None, None),
        P(),
        P(),
    )
    return jax.shard_map(
        body,
        mesh=mesh,
        in_specs=placed,
        out_specs=P(None, None, None, "vec", "space"),
        check_vma=False,
    )
```

time: 1160 us -> 94.5 us (0.08)
  waiting for transfers between devices: 1070 us -> 0 us
  Pallas kernels: 0 us -> 90.4 us
  local copies, waits for them, and re-layouts: 37 us -> 3.84 us
  starting transfers between devices: 20.6 us -> 0 us
  between operations: 14.1 us -> 0.01 us
    psum x1 -> x0, waiting for transfers between devices: 1020 us -> none  [body(): total = lax.psum(partial_value, 'space')]
    pallas_call x0 -> x1, Pallas kernels: none -> 90.4 us  [body(): pl.pallas_call(functools.partial(kernel, scale=scale), out_shape=jax.Shap...]
    ppermute x7 -> x0, waiting for transfers between devices: 42.9 us -> none  [the longest x5 42.9 us: passed_along(): lax.ppermute(shard, axis, [(i, (i + by) % devices) for i in range(devices)])]
    ppermute x7 -> x0, starting transfers between devices: 20.6 us -> none  [the longest x5 9.88 us: passed_along(): lax.ppermute(shard, axis, [(i, (i + by) % devices) for i in range(devices)])]
    mul x16 -> x0, local copies, waits for them, and re-layouts: 17.9 us -> none  [the longest x8 12.3 us: apply_link(): terms_re.append(link_re * vec_re - link_im * vec_im)]
  transfers between devices with their start and end apart: 8 -> 0, of which waited for: 4 -> 0; matrix products, arithmetic and copies ran while one was open for 4% -> 0% of each run, Pallas kernels for 0% -> 0%
where the time goes in v1:
time: 94.5 us; the launch traced here: 94.3 us
  Pallas kernels  90.4 us (96%)
  local copies, waits for them, and re-layouts  3.84 us (4%)
    pallas_call x1, Pallas kernels, body(): pl.pallas_call(functools.partial(kernel, scale=scale), out_shape=jax.Shap...  90.4 us
    unnamed x9, local copies, waits for them, and re-layouts  3.84 us

profile of v1, /device:TPU:1, one launch (start us, length us, event | category | flops | bytes accessed | tf_op | source)
XLA Modules:
  0.0 94.3 jit_solution(14030718277432024671)
XLA Ops:
  0.0 0.0 copy-start
  0.0 1.0 %copy-done = bf16[1,3,2,32,1024]{4,3,2,1,0:T(8,128)(2,1)S(1)} copy-done((bf16[1,3,2,32,1024]{4,3,2,1,0:T(8,128)(2,1)S(1)}, bf16[1,3,2,32,1024]{4,3,2,1,0:T(8,128)(2,1)}, u32[]{:S(2)}) %copy-start) | copy-done | bytes 393240
  1.0 0.0 copy-start.1
  1.0 0.9 copy-done.1
  1.9 0.0 copy-start.2
  1.9 0.7 copy-done.2
  2.6 0.0 copy-start.3
  2.6 0.7 copy-done.3
  3.2 90.4 %elementals.1 = f32[3,5,2,1,16]{4,3,2,1,0:T(1,128)S(1)} custom-call(bf16[1,3,2,32,1024]{4,3,2,1,0:T(8,128)(2,1)S(1)} %copy-done, f32[1,3,3,3,2,1024]{5,4,3,2,1,0:T(2,128)S(1)} %copy-done.1, s32[3]{0:T(128)S(1)} %copy-done.2, s32[5]{0:T(128)S(1)} %copy-done.3), custom_call_target="tpu_custom_call" | custom-call | tf_op jit(solution)/shard_map/elementals/pallas_call | solution.py:334
  93.7 0.6 copy.6
Async XLA Ops:
  0.0 1.0 %copy-start = (bf16[1,3,2,32,1024]{4,3,2,1,0:T(8,128)(2,1)S(1)}, bf16[1,3,2,32,1024]{4,3,2,1,0:T(8,128)(2,1)}, u32[]{:S(2)}) copy-start(bf16[1,3,2,32,1024]{4,3,2,1,0:T(8,128)(2,1)} %vec_hbm.1) | copy-start | bytes 1179652
  1.0 0.9 copy-start.1
  1.9 0.7 copy-start.2
  2.6 0.7 copy-start.3

commit v2 on v1

--- a/solution.py
+++ b/solution.py
@@ -86,26 +86,20 @@
     moved,
     shifted,
     acc,
-    tiles,
-    got_y,
-    sum_y,
-    got_x,
-    sum_x,
-    got_z,
-    sum_z,
-    got_c,
+    shares,
+    swapped,
+    sums,
+    arrived,
     picked,
     local_sem,
     ring_send,
     ring_recv,
     halo_send,
     halo_recv,
-    y_send,
-    y_recv,
-    x_send,
-    x_recv,
     pair_send,
     pair_recv,
+    share_send,
+    share_recv,
     *,
     scale,
 ):
@@ -126,10 +120,13 @@
     down = lax.rem(space + planes - 1, planes)
     after = lax.rem(vec + 1, nvec)
     before = lax.rem(vec + nvec - 1, nvec)
-    y_peers = [at(x, z_hi, lax.rem(y + i, NY), core) for i in range(1, NY)]
-    x_peers = [at(lax.rem(x + i, NX), z_hi, y, core) for i in range(1, NX)]
-    z_peer = at(x, 1 - z_hi, y, core)
-    c_peer = at(x, z_hi, y, 1 - core)
+    sibling = at(x, z_hi, y, 1 - core)
+
+    def peer_chip(j):
+        near = (j >= CHIPS // 2).astype(jnp.int32)
+        step = j - near * (CHIPS // 2 - 1)
+        dx, dy = lax.div(step, NY), lax.rem(step, NY)
+        return (lax.rem(x + dx, NX) * NH + lax.rem(z_hi + 1 - near, NH)) * NY + lax.rem(y + dy, NY)
 
     own = pltpu.make_async_copy(vec_hbm.at[0], blocks.at[0], local_sem.at[0])
     own.start()
@@ -137,12 +134,17 @@
     links_in.start()
 
     barrier = pltpu.get_barrier_semaphore()
-    peers = [up, down, z_peer] + y_peers + x_peers
-    for peer in peers:
+    def greet(j, carry):
+        peer = peer_chip(j) * NC + core
+        pl.semaphore_signal(barrier, inc=1, device_id={"space": peer}, device_id_type=pl.DeviceIdType.MESH)
+        return carry
+
+    for peer in (up, down):
         pl.semaphore_signal(barrier, inc=1, device_id={"space": peer}, device_id_type=pl.DeviceIdType.MESH)
     for peer in (after, before):
         pl.semaphore_signal(barrier, inc=1, device_id={"vec": peer}, device_id_type=pl.DeviceIdType.MESH)
-    pl.semaphore_wait(barrier, len(peers) + 2)
+    lax.fori_loop(0, CHIPS - 1, greet, 0)
+    pl.semaphore_wait(barrier, CHIPS + 3)
 
     def hop(k, c):
         return send(blocks.at[k, c], blocks.at[k + 1, c], ring_send.at[k, c], ring_recv.at[k, c], vec=after)
@@ -183,7 +185,10 @@
 
     def product(k, c, first, count):
         left = shifted[c, first : first + count, :]
-        right = blocks[k, c].reshape(2 * VB, SITES)
+        half = VB // 2
+        right = jnp.concatenate(
+            [blocks[k, c, q, h * half : (h + 1) * half, :] for h in range(NC) for q in range(2)], axis=0
+        )
         return lax.dot_general(left, right, (((1,), (1,)), ((), ())), preferred_element_type=jnp.float32)
 
     acc[...] = jnp.zeros_like(acc)
@@ -221,102 +226,73 @@
 
     lax.fori_loop(0, 3 * HOPS, x_step, 0)
 
+    def groups(k, h):
+        found = []
+        for mu in range(3):
+            first = acc[k, mu * 2 * VB : mu * 2 * VB + VB, :]
+            second = acc[k, mu * 2 * VB + VB : (mu + 1) * 2 * VB, :]
+            lane = h * VB
+            half = VB // 2
+            found.append(first[:, lane : lane + half] + second[:, lane + half : lane + VB])
+            found.append(first[:, lane + half : lane + VB] - second[:, lane : lane + half])
+        return found
+
+    for h in range(NC):
+        found = [g for k in range(HOPS) for g in groups(k, h)]
+        for j in range(3):
+            shares[h, :, j, :] = jnp.concatenate(found[8 * j : 8 * j + 8], axis=1)
+
     def last_step(c, carry):
         hop(HOPS - 1, c).wait_recv()
         add(HOPS, c, (0, 6 * VB))
         return carry
 
     lax.fori_loop(0, 3, last_step, 0)
-
-    wide = [[] for _ in range(6)]
-    tail = []
+    empty = jnp.zeros((VB, VB), jnp.float32)
+    for h in range(NC):
+        shares[h, :, 3, :] = jnp.concatenate(groups(HOPS, h) + [empty], axis=1)
+
+    swap = send(shares.at[1 - core], swapped, pair_send, pair_recv, space=sibling)
+    swap.start()
+    swap.wait_recv()
+    sums[...] = shares[core] + swapped[...]
+
+    def share(j):
+        dest = peer_chip(j)
+        return send(sums.at[dest], arrived.at[j], share_send.at[j], share_recv.at[j], space=dest * NC + core)
+
+    def share_start(j, carry):
+        share(j).start()
+        return carry
+
+    def share_add(j, total):
+        share(j).wait_recv()
+        return total + arrived[j]
+
+    lax.fori_loop(0, CHIPS - 1, share_start, 0)
+    total = lax.fori_loop(0, CHIPS - 1, share_add, sums[chip]) * scale
+
+    half = VB // 2
     for k in range(HOPS + 1):
-        for mu in range(3):
-            first = acc[k, mu * 2 * VB : mu * 2 * VB + VB, :]
-            second = acc[k, mu * 2 * VB + VB : (mu + 1) * 2 * VB, :]
-            real = first[:, :VB] + second[:, VB:]
-            imag = first[:, VB:] - second[:, :VB]
-            if k < HOPS:
-                wide[2 * mu].append(real)
-                wide[2 * mu + 1].append(imag)
-            else:
-                tail += [real, imag]
-    for j in range(6):
-        tiles[pl.ds(j, CHIPS, stride=8), :] = jnp.concatenate(wide[j], axis=1) * scale
-    tiles[pl.ds(6, CHIPS, stride=8), :] = jnp.concatenate(tail[:4], axis=1) * scale
-    empty = jnp.zeros((VB, 2 * VB), jnp.float32)
-    tiles[pl.ds(7, CHIPS, stride=8), :] = jnp.concatenate(tail[4:] + [empty], axis=1) * scale
-
-    sends = []
-
-    def tile(xx, hh, yy):
-        return pl.ds(pl.multiple_of(((xx * NH + hh) * NY + yy) * 8, 8), 8)
-
-    for i in range(1, NY):
-        yy = lax.rem(y + i, NY)
-        for g in range(NX * NH):
-            sends.append(
-                send(
-                    tiles.at[tile(0, g, yy)],
-                    got_y.at[i - 1, pl.ds(g * 8, 8)],
-                    y_send.at[i - 1, g],
-                    y_recv.at[i - 1, g],
-                    space=y_peers[i - 1],
-                )
-            )
-            sends[-1].start()
-    for copy in sends:
-        copy.wait_recv()
-    for g in range(NX * NH):
-        total = tiles[tile(0, g, y), :]
-        for i in range(NY - 1):
-            total = total + got_y[i, pl.ds(g * 8, 8), :]
-        sum_y[pl.ds(g * 8, 8), :] = total
-
-    x_sends = []
-    for i in range(1, NX):
-        xx = lax.rem(x + i, NX)
-        rows = pl.ds(pl.multiple_of(xx * NH * 8, 8), NH * 8)
-        x_sends.append(
-            send(sum_y.at[rows], got_x.at[i - 1], x_send.at[i - 1], x_recv.at[i - 1], space=x_peers[i - 1])
-        )
-        x_sends[-1].start()
-    for copy in x_sends:
-        copy.wait_recv()
-    total = sum_y[pl.ds(pl.multiple_of(x * NH * 8, 8), NH * 8), :]
-    for i in range(NX - 1):
-        total = total + got_x[i]
-    sum_x[...] = total
-
-    z_copy = send(
-        sum_x.at[pl.ds(pl.multiple_of((1 - z_hi) * 8, 8), 8)], got_z, pair_send.at[0], pair_recv.at[0], space=z_peer
-    )
-    z_copy.start()
-    z_copy.wait_recv()
-    sum_z[...] = sum_x[pl.ds(pl.multiple_of(z_hi * 8, 8), 8), :] + got_z[...]
-    c_copy = send(sum_z, got_c, pair_send.at[1], pair_recv.at[1], space=c_peer)
-    c_copy.start()
-    c_copy.wait_recv()
-    total = sum_z[...] + got_c[...]
-
-    half = VB // 2
-    for mu in range(3):
-        for t in range(2):
-            j = 2 * mu + t
-            for k in range(HOPS + 1):
-                row, lane = (j, k * VB) if k < HOPS else (6 + j // 4, (j % 4) * VB)
-                low = total[row : row + 1, lane : lane + half]
-                high = total[row : row + 1, lane + half : lane + VB]
-                at_row = (mu * (HOPS + 1) + k) * 2 + t
-                picked[at_row : at_row + 1, :half] = jnp.where(core == 0, low, high)
+        for j in range(6):
+            group = k * 6 + j
+            row, lane = group // 8, (group % 8) * half
+            at_row = ((j // 2) * (HOPS + 1) + k) * 2 + j % 2
+            picked[at_row : at_row + 1, :half] = total[row : row + 1, lane : lane + half]
     for d in range(3):
         mu = directions[d]
         for q in range(HOPS + 1):
             rows = pl.ds((mu * (HOPS + 1) + offsets[q]) * 2, 2)
             out[d, q, :, 0, :] = picked[rows, :half]
 
-    for copy in firsts + [to_up, to_down, link_up] + sends + x_sends + [z_copy, c_copy]:
+    for copy in firsts + [to_up, to_down, link_up, swap]:
         copy.wait_send()
+
+    def share_drain(j, carry):
+        share(j).wait_send()
+        return carry
+
+    lax.fori_loop(0, CHIPS - 1, share_drain, 0)
 
     def drain(i, carry):
         hop(lax.div(i, 3) + 1, lax.rem(i, 3)).wait_send()
@@ -351,29 +327,23 @@
             pltpu.VMEM((4,) + block, bf16),
             pltpu.VMEM((3, 6 * VB, SITES), bf16),
             pltpu.VMEM((HOPS + 1, 6 * VB, 2 * VB), f32),
-            pltpu.VMEM((CHIPS * 8, 128), f32),
-            pltpu.VMEM((NY - 1, NX * NH * 8, 128), f32),
-            pltpu.VMEM((NX * NH * 8, 128), f32),
-            pltpu.VMEM((NX - 1, NH * 8, 128), f32),
-            pltpu.VMEM((NH * 8, 128), f32),
-            pltpu.VMEM((8, 128), f32),
-            pltpu.VMEM((8, 128), f32),
-            pltpu.VMEM((8, 128), f32),
+            pltpu.VMEM((NC, CHIPS, 4, 128), f32),
+            pltpu.VMEM((CHIPS, 4, 128), f32),
+            pltpu.VMEM((CHIPS, 4, 128), f32),
+            pltpu.VMEM((CHIPS - 1, 4, 128), f32),
             pltpu.VMEM((6 * (HOPS + 1) + 2, 128), f32),
             dma((2,)),
             dma((HOPS, 3)),
             dma((HOPS, 3)),
             dma((3,)),
             dma((3,)),
-            dma((NY - 1, NX * NH)),
-            dma((NY - 1, NX * NH)),
-            dma((NX - 1,)),
-            dma((NX - 1,)),
-            dma((2,)),
-            dma((2,)),
+            dma,
+            dma,
+            dma((CHIPS - 1,)),
+            dma((CHIPS - 1,)),
         ],
         compiler_params=pltpu.CompilerParams(
-            collective_id=0, has_side_effects=True, vmem_limit_bytes=40 * 1024 * 1024
+            collective_id=0, has_side_effects=True, vmem_limit_bytes=63 * 1024 * 1024
         ),
         name="elementals",
     )(vectors, links, directions, offsets)

time: 94.5 us -> 90.8 us (0.961)
  local copies, waits for them, and re-layouts: 3.84 us -> 1.32 us
  Pallas kernels: 90.4 us -> 89.2 us
    unnamed x9 -> x1, local copies, waits for them, and re-layouts: 3.84 us -> 1.32 us
    pallas_call x1, Pallas kernels: 90.4 us -> 89.2 us  [body(): pl.pallas_call(functools.partial(kernel, scale=scale), out_shape=jax.Shap...]
where the time goes in v2:
time: 90.8 us; the launch traced here: 90.6 us
  Pallas kernels  89.2 us (98%)
  local copies, waits for them, and re-layouts  1.32 us (1%)
    pallas_call x1, Pallas kernels, body(): pl.pallas_call(functools.partial(kernel, scale=scale), out_shape=jax.Shap...  89.2 us

profile of v2, /device:TPU:1, one launch (start us, length us, event | category | flops | bytes accessed | tf_op | source)
XLA Modules:
  0.0 90.6 jit_solution(9846206735368991044)
XLA Ops:
  0.0 89.2 %elementals.1 = f32[3,5,2,1,16]{4,3,2,1,0:T(1,128)} custom-call(bf16[1,3,2,32,1024]{4,3,2,1,0:T(8,128)(2,1)} %vec_hbm.1, f32[1,3,3,3,2,1024]{5,4,3,2,1,0:T(2,128)} %link_hbm.1, s32[3]{0:T(128)} %directions.1, s32[5]{0:T(128)} %offsets.1), custom_call_target="tpu_custom_call" | custom-call | tf_op jit(solution)/shard_map/elementals/pallas_call | solution.py:310
  89.2 1.3 %copy.6 = f32[3,5,2,1,16]{4,3,2,1,0:T(1,128)} copy(f32[3,5,2,1,16]{4,3,2,1,0:T(1,128)} %elementals.1) | data formatting | bytes 3840

commit v3 on v0

v3 whole, which is shorter than its diff:
```python
import functools
import math

import jax
import jax.numpy as jnp
from jax import lax
from jax.experimental import pallas as pl
from jax.experimental.pallas import tpu as pltpu
from jax.sharding import PartitionSpec as P

LZ = 16
SITES = 1024
VB = 32
NV = 256
NB = NV // VB
NK = 5
CHUNK = SITES // NB
NX, NH, NY, NC = 4, 2, 4, 2
ROWS = NX * NH * NY


def send(src, dst, send_sem, recv_sem, **where):
    return pltpu.make_async_remote_copy(
        src_ref=src,
        dst_ref=dst,
        send_sem=send_sem,
        recv_sem=recv_sem,
        device_id=where,
        device_id_type=pl.DeviceIdType.MESH,
    )


def kernel(
    vec_hbm,
    link_hbm,
    directions,
    offsets,
    out,
    own,
    held,
    above,
    edges,
    edge,
    links,
    moved,
    phi,
    parts,
    swapped,
    got_y,
    sum_y,
    got_x,
    sum_x,
    got_z,
    both,
    picked,
    local_sem,
    vec_send,
    vec_recv,
    edge_send,
    edge_recv,
    halo_send,
    halo_recv,
    swap_send,
    swap_recv,
    y_send,
    y_recv,
    x_send,
    x_recv,
    z_send,
    z_recv,
    last_send,
    last_recv,
    *,
    scale,
):
    space = lax.axis_index("space")
    lane = lax.axis_index("vec")
    planes = lax.axis_size("space")
    core = lax.rem(space, NC)
    y = lax.rem(lax.div(space, NC), NY)
    z_hi = lax.rem(lax.div(space, NC * NY), NH)
    x = lax.div(space, NC * NY * NH)
    up = lax.rem(space + 1, planes)
    down = lax.rem(space + planes - 1, planes)

    def at(x, z_hi, y, core):
        return ((x * NH + z_hi) * NY + y) * NC + core

    def flip(z_hi, lane):
        return lane + z_hi * (NB - 1 - 2 * lane)

    def half_of(space):
        return lax.rem(lax.div(space, NC * NY), NH)

    chunk = flip(z_hi, lane)
    up_lane = flip(half_of(up), chunk)
    down_lane = flip(half_of(down), chunk)
    sibling = at(x, z_hi, y, 1 - core)

    def lanes_of(chunk):
        return pl.ds(pl.multiple_of(chunk * CHUNK, CHUNK), CHUNK)

    def rows_of(block):
        return pl.ds(pl.multiple_of(block * VB, VB), VB)

    own_in = pltpu.make_async_copy(vec_hbm.at[0], own, local_sem.at[0])
    links_in = pltpu.make_async_copy(link_hbm.at[0, :, :, :, :, lanes_of(chunk)], links, local_sem.at[1])
    mine_in = pltpu.make_async_copy(
        vec_hbm.at[0, :, :, :, lanes_of(chunk)], held.at[:, :, rows_of(lane), :], local_sem.at[2]
    )
    own_in.start()
    links_in.start()
    mine_in.start()

    def z_peer(j):
        near = (j >= NB).astype(jnp.int32)
        return lax.rem(z_hi + 1 - near, NH), lax.rem(lane + j + near, NB)

    barrier = pltpu.get_barrier_semaphore()

    def greet(space, lane):
        pl.semaphore_signal(
            barrier, inc=1, device_id={"space": space, "vec": lane}, device_id_type=pl.DeviceIdType.MESH
        )

    def greet_z(j, carry):
        there, peer = z_peer(j)
        greet(at(x, there, y, core), peer)
        return carry

    lax.fori_loop(0, NH * NB - 1, greet_z, 0)
    for i in range(1, NY):
        greet(at(x, z_hi, lax.rem(y + i, NY), core), lane)
    for i in range(1, NX):
        greet(at(lax.rem(x + i, NX), z_hi, y, core), lane)
    greet(up, up_lane)
    greet(down, down_lane)

    place = lax.broadcasted_iota(jnp.int32, (16, CHUNK), 1)
    own_in.wait()

    def pack(i, carry):
        to = lax.div(i, 2)
        rows = pl.ds(pl.multiple_of(lax.rem(i, 2) * 16, 16), 16)
        found = jnp.zeros((16, CHUNK), jnp.float32)
        for n in range(6):
            field = own[n // 2, n % 2, rows, lanes_of(lax.rem(to + 1, NB))].astype(jnp.float32)
            found = jnp.where(place // LZ == n, pltpu.roll(field, n * LZ, 1) if n else field, found)
        edges[to, rows, :] = found.astype(jnp.bfloat16)
        return carry

    lax.fori_loop(0, 2 * NB, pack, 0)
    edge[lane] = edges[chunk]
    mine_in.wait()
    links_in.wait()

    pl.semaphore_wait(barrier, NH * NB - 1 + NY - 1 + NX - 1 + 2)

    def piece(j):
        to = lax.rem(lane + j, NB)
        return send(
            vec_hbm.at[0, :, :, :, lanes_of(flip(z_hi, to))],
            held.at[:, :, rows_of(lane), :],
            vec_send.at[j - 1],
            vec_recv.at[j - 1],
            vec=to,
        )

    def edge_piece(j):
        to = lax.rem(lane + j, NB)
        return send(edges.at[flip(z_hi, to)], edge.at[lane], edge_send.at[j - 1], edge_recv.at[j - 1], vec=to)

    def from_lane(j):
        block = lax.rem(lane + NB - j, NB)
        return (
            send(held.at[:, :, rows_of(block), :], held.at[:, :, rows_of(block), :], vec_send.at[j - 1], vec_recv.at[j - 1], vec=block),
            send(edges.at[0], edge.at[block], edge_send.at[j - 1], edge_recv.at[j - 1], vec=block),
        )

    def start_pieces(j, carry):
        piece(j).start()
        return carry

    def start_edges(j, carry):
        edge_piece(j).start()
        return carry

    lax.fori_loop(1, NB, start_pieces, 0)
    lax.fori_loop(1, NB, start_edges, 0)

    def halo(block):
        rows = rows_of(block)
        return pltpu.make_async_remote_copy(
            src_ref=held.at[:, :, rows, :],
            dst_ref=above.at[:, :, rows, :],
            send_sem=halo_send.at[block],
            recv_sem=halo_recv.at[block],
            device_id={"space": down, "vec": down_lane},
            device_id_type=pl.DeviceIdType.MESH,
        )

    def forward(mu, rows, vecs):
        for row in range(3):
            real = []
            imag = []
            for col in range(3):
                link_re = links[mu, row, col, pl.ds(0, 1), :]
                link_im = links[mu, row, col, pl.ds(1, 1), :]
                vec_re, vec_im = vecs[col]
                real.append(link_re * vec_re - link_im * vec_im)
                imag.append(link_re * vec_im + link_im * vec_re)
            moved[mu, row, 0, rows, :] = (real[0] + real[1] + real[2]).astype(jnp.bfloat16)
            moved[mu, row, 1, rows, :] = (imag[0] + imag[1] + imag[2]).astype(jnp.bfloat16)

    def move_yz(block):
        def step(i, carry):
            first = pl.multiple_of(i * 16, 16)
            rows = pl.ds(pl.multiple_of(block * VB + first, 16), 16)
            vecs = [[held[c, p, rows, :].astype(jnp.float32) for p in range(2)] for c in range(3)]
            border = edge[block, pl.ds(first, 16), :].astype(jnp.float32)
            along_y = [
                [
                    jnp.where(
                        place < CHUNK - LZ,
                        pltpu.roll(vecs[c][p], CHUNK - LZ, 1),
                        pltpu.roll(border, CHUNK - LZ - LZ * (2 * c + p), 1),
                    )
                    for p in range(2)
                ]
                for c in range(3)
            ]
            forward(1, rows, along_y)
            along_z = [
                [
                    jnp.where(place % LZ == LZ - 1, pltpu.roll(v, LZ - 1, 1), pltpu.roll(v, CHUNK - 1, 1))
                    for v in vecs[c]
                ]
                for c in range(3)
            ]
            forward(2, rows, along_z)
            return carry

        lax.fori_loop(0, 2, step, 0)

    def move_x(block):
        def step(i, carry):
            rows = pl.ds(pl.multiple_of(block * VB + i * 16, 16), 16)
            forward(0, rows, [[above[c, p, rows, :].astype(jnp.float32) for p in range(2)] for c in range(3)])
            return carry

        lax.fori_loop(0, 2, step, 0)

    halo(lane).start()
    move_yz(lane)

    def arrive(j, carry):
        block = lax.rem(lane + NB - j, NB)
        for copy in from_lane(j):
            copy.wait_recv()
        halo(block).start()
        move_yz(block)
        return carry

    lax.fori_loop(1, NB, arrive, 0)

    def product(mu):
        left = [
            jnp.concatenate([moved[mu, c, p] for c in range(3)] + [held[c, p] for c in range(3)], axis=1)
            for p in range(2)
        ]
        right = [
            jnp.concatenate([held[c, p] for c in range(3)] + [moved[mu, c, p] for c in range(3)], axis=1)
            for p in range(2)
        ]

        def dot(p, q):
            return lax.dot_general(
                left[p], right[q], (((1,), (1,)), ((), ())), preferred_element_type=jnp.float32
            )

        for t, total in enumerate((dot(0, 0) + dot(1, 1), dot(0, 1) - dot(1, 0))):
            for n in range(2):
                phi[mu, t, n] = total[:, n * 128 : (n + 1) * 128]

    product(1)
    product(2)

    def arrive_x(j, carry):
        block = lax.rem(up_lane + NB - j, NB)
        halo(block).wait_recv()
        move_x(block)
        return carry

    lax.fori_loop(0, NB, arrive_x, 0)
    product(0)

    wide = lax.broadcasted_iota(jnp.int32, (8, 128), 1)
    for t in range(2):
        for a in range(NB):
            turn = ((a + NB - 3) % NB) * VB
            for yy in range(NY):
                last = []
                for mu in range(3):
                    first, second = (
                        phi[mu, t, (n + turn // 128) % 2, pl.ds(a * VB + yy, 8, stride=NY), :] for n in range(2)
                    )
                    stay = 128 - turn % 128
                    if stay < 128:
                        first, second = pltpu.roll(first, stay, 1), pltpu.roll(second, stay, 1)
                        first, second = jnp.where(wide < stay, first, second), jnp.where(wide < stay, second, first)
                    parts[t, yy, mu, pl.ds(a, 8, stride=8), :] = first
                    shift = (mu * VB + VB) % 128
                    last.append(pltpu.roll(second, shift, 1))
                parts[t, yy, 3, pl.ds(a, 8, stride=8), :] = jnp.where(
                    wide < VB, last[0], jnp.where(wide < 2 * VB, last[1], last[2])
                )

    def swap(i):
        yy = lax.rem(y + i, NY)
        return send(parts.at[1 - core, yy], swapped.at[yy], swap_send.at[yy], swap_recv.at[yy], space=sibling)

    def to_y(i):
        yy = lax.rem(y + i, NY)
        return send(
            parts.at[core, yy], got_y.at[i - 1], y_send.at[i - 1], y_recv.at[i - 1], space=at(x, z_hi, yy, core)
        )

    def swap_start(i, carry):
        swap(i).start()
        return carry

    lax.fori_loop(1, NY + 1, swap_start, 0)

    def swap_add(i):
        yy = lax.rem(y + i, NY)
        swap(i).wait_recv()
        parts[core, yy] = parts[core, yy] + swapped[yy]

    def y_start(i, carry):
        swap_add(i)
        to_y(i).start()
        return carry

    lax.fori_loop(1, NY, y_start, 0)
    swap_add(NY)
    for i in range(1, NY):
        to_y(i).wait_recv()
    for b in range(4):
        for xx in range(NX):
            rows = pl.ds(xx * 16, 16)
            total = parts[core, y, b, rows, :]
            for i in range(NY - 1):
                total = total + got_y[i, b, rows, :]
            sum_y[xx, b] = total

    def to_x(i):
        xx = lax.rem(x + i, NX)
        return send(sum_y.at[xx], got_x.at[i - 1], x_send.at[i - 1], x_recv.at[i - 1], space=at(xx, z_hi, y, core))

    for i in range(1, NX):
        to_x(i).start()
    for i in range(1, NX):
        to_x(i).wait_recv()
    for b in range(4):
        total = sum_y[x, b]
        for i in range(NX - 1):
            total = total + got_x[i, b]
        sum_x[:, b, :] = total

    def to_z(j):
        there, peer = z_peer(j)
        return pltpu.make_async_remote_copy(
            src_ref=sum_x.at[there * NB + peer],
            dst_ref=got_z.at[j],
            send_sem=z_send.at[j],
            recv_sem=z_recv.at[j],
            device_id={"space": at(x, there, y, core), "vec": peer},
            device_id_type=pl.DeviceIdType.MESH,
        )

    def z_start(j, carry):
        to_z(j).start()
        return carry

    def z_add(j, total):
        to_z(j).wait_recv()
        return total + got_z[j]

    lax.fori_loop(0, NH * NB - 1, z_start, 0)
    both[core] = lax.fori_loop(0, NH * NB - 1, z_add, sum_x[z_hi * NB + lane]) * scale
    last = send(both.at[core], both.at[core], last_send, last_recv, space=sibling)
    last.start()
    last_in = send(both.at[1 - core], both.at[1 - core], last_send, last_recv, space=sibling)
    last_in.wait_recv()

    half = VB // 2
    for t in range(2):
        total = both[t]
        for mu in range(3):
            for k in range(NK):
                row, first = (mu, (3 - k) * VB) if k < 4 else (3, mu * VB)
                low = total[row : row + 1, first : first + half]
                high = total[row : row + 1, first + half : first + VB]
                at_row = (mu * NK + k) * 2 + t
                picked[at_row : at_row + 1, :half] = jnp.where(core == 0, low, high)
    for d in range(3):
        mu = directions[d]
        for q in range(NK):
            rows = pl.ds((mu * NK + offsets[q]) * 2, 2)
            out[d, q, :, 0, :] = picked[rows, :half]

    def drain(j, carry):
        piece(j).wait_send()
        edge_piece(j).wait_send()
        return carry

    def drain_halo(block, carry):
        halo(block).wait_send()
        return carry

    def drain_z(j, carry):
        to_z(j).wait_send()
        return carry

    lax.fori_loop(1, NB, drain, 0)
    lax.fori_loop(0, NB, drain_halo, 0)
    for i in range(1, NY + 1):
        swap(i).wait_send()
    for i in range(1, NY):
        to_y(i).wait_send()
    for i in range(1, NX):
        to_x(i).wait_send()
    lax.fori_loop(0, NH * NB - 1, drain_z, 0)
    last.wait_send()


def body(vectors, links, directions, offsets):
    planes = lax.axis_size("space")
    scale = 1.0 / math.sqrt(6.0 * planes * SITES)
    bf16, f32 = jnp.bfloat16, jnp.float32
    dma = pltpu.SemaphoreType.DMA
    zs = NH * NB - 1
    return pl.pallas_call(
        functools.partial(kernel, scale=scale),
        out_shape=jax.ShapeDtypeStruct((3, NK, 2, 1, VB // 2), f32),
        in_specs=[
            pl.BlockSpec(memory_space=pl.ANY),
            pl.BlockSpec(memory_space=pl.ANY),
            pl.BlockSpec(memory_space=pltpu.SMEM),
            pl.BlockSpec(memory_space=pltpu.SMEM),
        ],
        out_specs=pl.BlockSpec(memory_space=pltpu.VMEM),
        scratch_shapes=[
            pltpu.VMEM((3, 2, VB, SITES), bf16),
            pltpu.VMEM((3, 2, NV, CHUNK), bf16),
            pltpu.VMEM((3, 2, NV, CHUNK), bf16),
            pltpu.VMEM((NB, VB, CHUNK), bf16),
            pltpu.VMEM((NB, VB, CHUNK), bf16),
            pltpu.VMEM((3, 3, 3, 2, CHUNK), f32),
            pltpu.VMEM((3, 3, 2, NV, CHUNK), bf16),
            pltpu.VMEM((3, 2, 2, NV, 128), f32),
            pltpu.VMEM((2, NY, 4, 64, 128), f32),
            pltpu.VMEM((NY, 4, 64, 128), f32),
            pltpu.VMEM((NY - 1, 4, 64, 128), f32),
            pltpu.VMEM((NX, 4, 16, 128), f32),
            pltpu.VMEM((NX - 1, 4, 16, 128), f32),
            pltpu.VMEM((16, 4, 128), f32),
            pltpu.VMEM((zs, 4, 128), f32),
            pltpu.VMEM((2, 4, 128), f32),
            pltpu.VMEM((6 * NK + 2, 128), f32),
            dma((3,)),
            dma((NB - 1,)),
            dma((NB - 1,)),
            dma((NB - 1,)),
            dma((NB - 1,)),
            dma((NB,)),
            dma((NB,)),
            dma((NY,)),
            dma((NY,)),
            dma((NY - 1,)),
            dma((NY - 1,)),
            dma((NX - 1,)),
            dma((NX - 1,)),
            dma((zs,)),
            dma((zs,)),
            dma,
            dma,
        ],
        compiler_params=pltpu.CompilerParams(
            collective_id=0, has_side_effects=True, vmem_limit_bytes=63 * 1024 * 1024
        ),
        name="elementals",
    )(vectors, links, directions, offsets)


def solution(mesh):
    placed = (
        P("space", None, None, "vec", None),
        P("space", None, None, None, None, None),
        P(),
        P(),
    )
    return jax.shard_map(
        body,
        mesh=mesh,
        in_specs=placed,
        out_specs=P(None, None, None, "vec", "space"),
        check_vma=False,
    )
```

time: 1160 us -> 83.6 us (0.07)
  waiting for transfers between devices: 1070 us -> 0 us
  Pallas kernels: 0 us -> 81.9 us
  local copies, waits for them, and re-layouts: 37 us -> 1.32 us
  starting transfers between devices: 20.6 us -> 0 us
  between operations: 14.1 us -> 0.01 us
    psum x1 -> x0, waiting for transfers between devices: 1020 us -> none  [body(): total = lax.psum(partial_value, 'space')]
    pallas_call x0 -> x1, Pallas kernels: none -> 81.9 us  [body(): pl.pallas_call(functools.partial(kernel, scale=scale), out_shape=jax.Shap...]
    ppermute x7 -> x0, waiting for transfers between devices: 42.9 us -> none  [the longest x5 42.9 us: passed_along(): lax.ppermute(shard, axis, [(i, (i + by) % devices) for i in range(devices)])]
    ppermute x7 -> x0, starting transfers between devices: 20.6 us -> none  [the longest x5 9.88 us: passed_along(): lax.ppermute(shard, axis, [(i, (i + by) % devices) for i in range(devices)])]
    mul x16 -> x0, local copies, waits for them, and re-layouts: 17.9 us -> none  [the longest x8 12.3 us: apply_link(): terms_re.append(link_re * vec_re - link_im * vec_im)]
  transfers between devices with their start and end apart: 8 -> 0, of which waited for: 4 -> 0; matrix products, arithmetic and copies ran while one was open for 4% -> 0% of each run, Pallas kernels for 0% -> 0%
where the time goes in v3:
time: 83.6 us; the launch traced here: 83.2 us
  Pallas kernels  81.9 us (98%)
  local copies, waits for them, and re-layouts  1.32 us (2%)
    pallas_call x1, Pallas kernels, body(): pl.pallas_call(functools.partial(kernel, scale=scale), out_shape=jax.Shap...  81.9 us

profile of v3, /device:TPU:1, one launch (start us, length us, event | category | flops | bytes accessed | tf_op | source)
XLA Modules:
  0.0 83.2 jit_solution(8387114922507385443)
XLA Ops:
  0.0 81.9 %elementals.1 = f32[3,5,2,1,16]{4,3,2,1,0:T(1,128)} custom-call(bf16[1,3,2,32,1024]{4,3,2,1,0:T(8,128)(2,1)} %vec_hbm.1, f32[1,3,3,3,2,1024]{5,4,3,2,1,0:T(2,128)} %link_hbm.1, s32[3]{0:T(128)} %directions.1, s32[5]{0:T(128)} %offsets.1), custom_call_target="tpu_custom_call" | custom-call | tf_op jit(solution)/shard_map/elementals/pallas_call | solution.py:443
  81.9 1.3 %copy.6 = f32[3,5,2,1,16]{4,3,2,1,0:T(1,128)} copy(f32[3,5,2,1,16]{4,3,2,1,0:T(1,128)} %elementals.1) | data formatting | bytes 3840

commit v4 on v3

--- a/solution.py
+++ b/solution.py
@@ -39,6 +39,7 @@
     own,
     held,
     above,
+    hold,
     edges,
     edge,
     links,
@@ -46,10 +47,8 @@
     phi,
     parts,
     swapped,
-    got_y,
-    sum_y,
-    got_x,
-    sum_x,
+    got_xy,
+    sum_xy,
     got_z,
     both,
     picked,
@@ -60,12 +59,12 @@
     edge_recv,
     halo_send,
     halo_recv,
+    hold_send,
+    hold_recv,
     swap_send,
     swap_recv,
-    y_send,
-    y_recv,
-    x_send,
-    x_recv,
+    xy_send,
+    xy_recv,
     z_send,
     z_recv,
     last_send,
@@ -129,12 +128,21 @@
         return carry
 
     lax.fori_loop(0, NH * NB - 1, greet_z, 0)
-    for i in range(1, NY):
-        greet(at(x, z_hi, lax.rem(y + i, NY), core), lane)
-    for i in range(1, NX):
-        greet(at(lax.rem(x + i, NX), z_hi, y, core), lane)
+    for i in range(1, NX * NY):
+        greet(at(lax.rem(x + i % NX, NX), z_hi, lax.rem(y + i // NX, NY), core), lane)
     greet(up, up_lane)
     greet(down, down_lane)
+
+    crossing = jnp.logical_and(y == 0, core == 0)
+    crossed = jnp.logical_and(y == NY - 1, core == NC - 1)
+    relays = jnp.logical_and(y > 0, core == 0)
+    beyond = lax.rem(at(x, z_hi, 0, 0) + planes - 1, planes)
+    beyond_lane = flip(half_of(beyond), chunk)
+
+    @pl.when(crossed)
+    def _():
+        for q in range(1, NY):
+            greet(up + q * NC, up_lane)
 
     place = lax.broadcasted_iota(jnp.int32, (16, CHUNK), 1)
     own_in.wait()
@@ -154,7 +162,7 @@
     mine_in.wait()
     links_in.wait()
 
-    pl.semaphore_wait(barrier, NH * NB - 1 + NY - 1 + NX - 1 + 2)
+    pl.semaphore_wait(barrier, NH * NB - 1 + NX * NY - 1 + 2 + relays.astype(jnp.int32))
 
     def piece(j):
         to = lax.rem(lane + j, NB)
@@ -198,6 +206,42 @@
             device_id={"space": down, "vec": down_lane},
             device_id_type=pl.DeviceIdType.MESH,
         )
+
+    def to_relay(j, block):
+        n = lax.div(j, NY)
+        return send(
+            held.at[:, :, rows_of(block), :],
+            hold.at[n],
+            halo_send.at[block],
+            hold_recv.at[n],
+            space=at(x, z_hi, lax.rem(j, NY), core),
+        )
+
+    def start_halo(j, block):
+        aside = jnp.logical_and(crossing, lax.rem(j, NY) != 0)
+
+        @pl.when(aside)
+        def _():
+            to_relay(j, block).start()
+
+        @pl.when(jnp.logical_not(aside))
+        def _():
+            halo(block).start()
+
+    def handed(n):
+        block = lax.rem(lane + 2 * NB - y - n * NY, NB)
+        return pltpu.make_async_remote_copy(
+            src_ref=hold.at[n],
+            dst_ref=above.at[:, :, rows_of(block), :],
+            send_sem=hold_send.at[n],
+            recv_sem=halo_recv.at[block],
+            device_id={"space": beyond, "vec": beyond_lane},
+            device_id_type=pl.DeviceIdType.MESH,
+        )
+
+    def hand_on(n):
+        send(hold.at[n], hold.at[n], hold_send.at[n], hold_recv.at[n], space=sibling).wait_recv()
+        handed(n).start()
 
     def forward(mu, rows, vecs):
         for row in range(3):
@@ -250,18 +294,28 @@
 
         lax.fori_loop(0, 2, step, 0)
 
-    halo(lane).start()
+    start_halo(0, lane)
     move_yz(lane)
 
     def arrive(j, carry):
         block = lax.rem(lane + NB - j, NB)
         for copy in from_lane(j):
             copy.wait_recv()
-        halo(block).start()
+        start_halo(j, block)
         move_yz(block)
+
+        @pl.when(jnp.logical_and(jnp.logical_and(relays, j > 2), lax.rem(j + 2, NY) == y))
+        def _():
+            hand_on(lax.div(j - 2, NY))
+
         return carry
 
     lax.fori_loop(1, NB, arrive, 0)
+
+    @pl.when(jnp.logical_and(relays, y > 1))
+    def _():
+        hand_on(1)
+
 
     def product(mu):
         left = [
@@ -282,8 +336,98 @@
             for n in range(2):
                 phi[mu, t, n] = total[:, n * 128 : (n + 1) * 128]
 
+    wide = lax.broadcasted_iota(jnp.int32, (8, 128), 1)
+
+    def turned(mu, t, a, yy):
+        turn = ((a + NB - 3) % NB) * VB
+        first, second = (phi[mu, t, (n + turn // 128) % 2, pl.ds(a * VB + yy, 8, stride=NY), :] for n in range(2))
+        stay = 128 - turn % 128
+        if stay < 128:
+            first, second = pltpu.roll(first, stay, 1), pltpu.roll(second, stay, 1)
+            first, second = jnp.where(wide < stay, first, second), jnp.where(wide < stay, second, first)
+        return first, second
+
+    def lay(which, t, yy, b, a, rows):
+        for xx in range(NX):
+            parts[which, t, yy, xx, b, pl.ds(a, NH, stride=NB), :] = rows[NH * xx : NH * (xx + 1)]
+
+    def lay_first():
+        for t in range(2):
+            for a in range(NB):
+                for yy in range(NY):
+                    for b in range(2):
+                        lay(0, t, yy, b, a, turned(b + 1, t, a, yy)[0])
+
+    def lay_second():
+        for t in range(2):
+            for a in range(NB):
+                for yy in range(NY):
+                    last = []
+                    for mu in range(3):
+                        first, second = turned(mu, t, a, yy)
+                        if mu == 0:
+                            lay(1, t, yy, 0, a, first)
+                        last.append(pltpu.roll(second, (mu * VB + VB) % 128, 1))
+                    lay(1, t, yy, 1, a, jnp.where(wide < VB, last[0], jnp.where(wide < 2 * VB, last[1], last[2])))
+
+    def swap(which, i):
+        yy = lax.rem(y + i, NY)
+        return send(
+            parts.at[which, 1 - core, yy],
+            swapped.at[which, yy],
+            swap_send.at[which, yy],
+            swap_recv.at[which, yy],
+            space=sibling,
+        )
+
+    def to_xy(which, i, j):
+        yy, xx = lax.rem(y + i, NY), lax.rem(x + j, NX)
+        slot = lax.rem(i, NY) * NX + j - 1
+        return send(
+            parts.at[which, core, yy, xx],
+            got_xy.at[which, slot],
+            xy_send.at[which, slot],
+            xy_recv.at[which, slot],
+            space=at(xx, z_hi, yy, core),
+        )
+
+    def sum_cores(which):
+        def swap_start(i, carry):
+            swap(which, i).start()
+            return carry
+
+        def swap_add(i):
+            yy = lax.rem(y + i, NY)
+            swap(which, i).wait_recv()
+            parts[which, core, yy] = parts[which, core, yy] + swapped[which, yy]
+
+        def xy_start(i, carry):
+            swap_add(i)
+            for j in range(NX):
+                to_xy(which, i, j).start()
+            return carry
+
+        lax.fori_loop(1, NY + 1, swap_start, 0)
+        lax.fori_loop(1, NY, xy_start, 0)
+        swap_add(NY)
+        for j in range(1, NX):
+            to_xy(which, 0, j).start()
+
+    def sum_chips(which):
+        def xy_add(slot, totals):
+            i, j = lax.div(slot + 1, NX), lax.rem(slot + 1, NX)
+            to_xy(which, i, j).wait_recv()
+            return tuple(totals[b] + got_xy[which, slot, b] for b in range(2))
+
+        own_part = tuple(parts[which, core, y, x, b] for b in range(2))
+        totals = lax.fori_loop(0, NX * NY - 1, xy_add, own_part)
+        for b in range(2):
+            sum_xy[:, 2 * which + b, :] = totals[b]
+
     product(1)
     product(2)
+    lay_first()
+    sum_cores(0)
 
     def arrive_x(j, carry):
         block = lax.rem(up_lane + NB - j, NB)
@@ -293,84 +437,15 @@
 
     lax.fori_loop(0, NB, arrive_x, 0)
     product(0)
-
-    wide = lax.broadcasted_iota(jnp.int32, (8, 128), 1)
-    for t in range(2):
-        for a in range(NB):
-            turn = ((a + NB - 3) % NB) * VB
-            for yy in range(NY):
-                last = []
-                for mu in range(3):
-                    first, second = (
-                        phi[mu, t, (n + turn // 128) % 2, pl.ds(a * VB + yy, 8, stride=NY), :] for n in range(2)
-                    )
-                    stay = 128 - turn % 128
-                    if stay < 128:
-                        first, second = pltpu.roll(first, stay, 1), pltpu.roll(second, stay, 1)
-                        first, second = jnp.where(wide < stay, first, second), jnp.where(wide < stay, second, first)
-                    parts[t, yy, mu, pl.ds(a, 8, stride=8), :] = first
-                    shift = (mu * VB + VB) % 128
-                    last.append(pltpu.roll(second, shift, 1))
-                parts[t, yy, 3, pl.ds(a, 8, stride=8), :] = jnp.where(
-                    wide < VB, last[0], jnp.where(wide < 2 * VB, last[1], last[2])
-                )
-
-    def swap(i):
-        yy = lax.rem(y + i, NY)
-        return send(parts.at[1 - core, yy], swapped.at[yy], swap_send.at[yy], swap_recv.at[yy], space=sibling)
-
-    def to_y(i):
-        yy = lax.rem(y + i, NY)
-        return send(
-            parts.at[core, yy], got_y.at[i - 1], y_send.at[i - 1], y_recv.at[i - 1], space=at(x, z_hi, yy, core)
-        )
-
-    def swap_start(i, carry):
-        swap(i).start()
-        return carry
-
-    lax.fori_loop(1, NY + 1, swap_start, 0)
-
-    def swap_add(i):
-        yy = lax.rem(y + i, NY)
-        swap(i).wait_recv()
-        parts[core, yy] = parts[core, yy] + swapped[yy]
-
-    def y_start(i, carry):
-        swap_add(i)
-        to_y(i).start()
-        return carry
-
-    lax.fori_loop(1, NY, y_start, 0)
-    swap_add(NY)
-    for i in range(1, NY):
-        to_y(i).wait_recv()
-    for b in range(4):
-        for xx in range(NX):
-            rows = pl.ds(xx * 16, 16)
-            total = parts[core, y, b, rows, :]
-            for i in range(NY - 1):
-                total = total + got_y[i, b, rows, :]
-            sum_y[xx, b] = total
-
-    def to_x(i):
-        xx = lax.rem(x + i, NX)
-        return send(sum_y.at[xx], got_x.at[i - 1], x_send.at[i - 1], x_recv.at[i - 1], space=at(xx, z_hi, y, core))
-
-    for i in range(1, NX):
-        to_x(i).start()
-    for i in range(1, NX):
-        to_x(i).wait_recv()
-    for b in range(4):
-        total = sum_y[x, b]
-        for i in range(NX - 1):
-            total = total + got_x[i, b]
-        sum_x[:, b, :] = total
+    lay_second()
+    sum_cores(1)
+    sum_chips(0)
+    sum_chips(1)
 
     def to_z(j):
         there, peer = z_peer(j)
         return pltpu.make_async_remote_copy(
-            src_ref=sum_x.at[there * NB + peer],
+            src_ref=sum_xy.at[there * NB + peer],
             dst_ref=got_z.at[j],
             send_sem=z_send.at[j],
             recv_sem=z_recv.at[j],
@@ -387,7 +462,7 @@
         return total + got_z[j]
 
     lax.fori_loop(0, NH * NB - 1, z_start, 0)
-    both[core] = lax.fori_loop(0, NH * NB - 1, z_add, sum_x[z_hi * NB + lane]) * scale
+    both[core] = lax.fori_loop(0, NH * NB - 1, z_add, sum_xy[z_hi * NB + lane]) * scale
     last = send(both.at[core], both.at[core], last_send, last_recv, space=sibling)
     last.start()
     last_in = send(both.at[1 - core], both.at[1 - core], last_send, last_recv, space=sibling)
@@ -398,7 +473,7 @@
         total = both[t]
         for mu in range(3):
             for k in range(NK):
-                row, first = (mu, (3 - k) * VB) if k < 4 else (3, mu * VB)
+                row, first = ((mu + 2) % 3, (3 - k) * VB) if k < 4 else (3, mu * VB)
                 low = total[row : row + 1, first : first + half]
                 high = total[row : row + 1, first + half : first + VB]
                 at_row = (mu * NK + k) * 2 + t
@@ -418,18 +493,29 @@
         halo(block).wait_send()
         return carry
 
+    @pl.when(relays)
+    def _():
+        for n in range(2):
+            handed(n).wait_send()
+
     def drain_z(j, carry):
         to_z(j).wait_send()
         return carry
 
     lax.fori_loop(1, NB, drain, 0)
     lax.fori_loop(0, NB, drain_halo, 0)
-    for i in range(1, NY + 1):
-        swap(i).wait_send()
-    for i in range(1, NY):
-        to_y(i).wait_send()
-    for i in range(1, NX):
-        to_x(i).wait_send()
+    for which in range(2):
+
+        def drain_swap(i, carry):
+            swap(which, i).wait_send()
+            return carry
+
+        def drain_xy(slot, carry):
+            to_xy(which, lax.div(slot + 1, NX), lax.rem(slot + 1, NX)).wait_send()
+            return carry
+
+        lax.fori_loop(1, NY + 1, drain_swap, 0)
+        lax.fori_loop(0, NX * NY - 1, drain_xy, 0)
     lax.fori_loop(0, NH * NB - 1, drain_z, 0)
     last.wait_send()
 
@@ -454,16 +540,15 @@
             pltpu.VMEM((3, 2, VB, SITES), bf16),
             pltpu.VMEM((3, 2, NV, CHUNK), bf16),
             pltpu.VMEM((3, 2, NV, CHUNK), bf16),
+            pltpu.VMEM((2, 3, 2, VB, CHUNK), bf16),
             pltpu.VMEM((NB, VB, CHUNK), bf16),
             pltpu.VMEM((NB, VB, CHUNK), bf16),
             pltpu.VMEM((3, 3, 3, 2, CHUNK), f32),
             pltpu.VMEM((3, 3, 2, NV, CHUNK), bf16),
             pltpu.VMEM((3, 2, 2, NV, 128), f32),
-            pltpu.VMEM((2, NY, 4, 64, 128), f32),
-            pltpu.VMEM((NY, 4, 64, 128), f32),
-            pltpu.VMEM((NY - 1, 4, 64, 128), f32),
-            pltpu.VMEM((NX, 4, 16, 128), f32),
-            pltpu.VMEM((NX - 1, 4, 16, 128), f32),
+            pltpu.VMEM((2, 2, NY, NX, 2, 16, 128), f32),
+            pltpu.VMEM((2, NY, NX, 2, 16, 128), f32),
+            pltpu.VMEM((2, NX * NY - 1, 2, 16, 128), f32),
             pltpu.VMEM((16, 4, 128), f32),
             pltpu.VMEM((zs, 4, 128), f32),
             pltpu.VMEM((2, 4, 128), f32),
@@ -475,12 +560,12 @@
             dma((NB - 1,)),
             dma((NB,)),
             dma((NB,)),
-            dma((NY,)),
-            dma((NY,)),
-            dma((NY - 1,)),
-            dma((NY - 1,)),
-            dma((NX - 1,)),
-            dma((NX - 1,)),
+            dma((2,)),
+            dma((2,)),
+            dma((2, NY)),
+            dma((2, NY)),
+            dma((2, NX * NY - 1)),
+            dma((2, NX * NY - 1)),
             dma((zs,)),
             dma((zs,)),
             dma,

time: 83.6 us -> 74.9 us (0.90)
  Pallas kernels: 81.9 us -> 73.4 us
    pallas_call x1, Pallas kernels: 81.9 us -> 73.4 us  [body(): pl.pallas_call(functools.partial(kernel, scale=scale), out_shape=jax.Shap...]
where the time goes in v4:
time: 74.9 us; the launch traced here: 74.7 us
  Pallas kernels  73.4 us (98%)
  local copies, waits for them, and re-layouts  1.32 us (2%)
    pallas_call x1, Pallas kernels, body(): pl.pallas_call(functools.partial(kernel, scale=scale), out_shape=jax.Shap...  73.4 us

profile of v4, /device:TPU:1, one launch (start us, length us, event | category | flops | bytes accessed | tf_op | source)
XLA Modules:
  0.0 74.7 jit_solution(8984810020963815363)
XLA Ops:
  0.0 73.4 %elementals.1 = f32[3,5,2,1,16]{4,3,2,1,0:T(1,128)} custom-call(bf16[1,3,2,32,1024]{4,3,2,1,0:T(8,128)(2,1)} %vec_hbm.1, f32[1,3,3,3,2,1024]{5,4,3,2,1,0:T(2,128)} %link_hbm.1, s32[3]{0:T(128)} %directions.1, s32[5]{0:T(128)} %offsets.1), custom_call_target="tpu_custom_call" | custom-call | tf_op jit(solution)/shard_map/elementals/pallas_call | solution.py:529
  73.4 1.3 %copy.6 = f32[3,5,2,1,16]{4,3,2,1,0:T(1,128)} copy(f32[3,5,2,1,16]{4,3,2,1,0:T(1,128)} %elementals.1) | data formatting | bytes 3840

commit v5 on v4

--- a/solution.py
+++ b/solution.py
@@ -13,6 +13,7 @@
 VB = 32
 NV = 256
 NB = NV // VB
+WINDOW = 7
 NK = 5
 CHUNK = SITES // NB
 NX, NH, NY, NC = 4, 2, 4, 2
@@ -44,7 +45,9 @@
     edge,
     links,
     moved,
-    phi,
+    order,
+    ordered,
+    far,
     parts,
     swapped,
     got_xy,
@@ -144,7 +147,49 @@
         for q in range(1, NY):
             greet(up + q * NC, up_lane)
 
+    pl.semaphore_wait(barrier, NH * NB - 1 + NX * NY - 1 + 2 + relays.astype(jnp.int32))
+
+    def step_of(n):
+        if isinstance(n, int):
+            return (NB // 2 + (2 * (n % 2) - 1) * (n // 2)) if n else 0
+        return (n > 0).astype(jnp.int32) * (NB // 2 + (2 * lax.rem(n, 2) - 1) * lax.div(n, 2))
+
+    def block_of(lane, n):
+        return lax.rem(lane + NB - step_of(n), NB)
+
+    def piece(j):
+        to = lax.rem(lane + j, NB)
+        return send(
+            vec_hbm.at[0, :, :, :, lanes_of(flip(z_hi, to))],
+            held.at[:, :, rows_of(lane), :],
+            vec_send.at[j - 1],
+            vec_recv.at[j - 1],
+            vec=to,
+        )
+
+    def edge_piece(j):
+        to = lax.rem(lane + j, NB)
+        return send(edges.at[flip(z_hi, to)], edge.at[lane], edge_send.at[j - 1], edge_recv.at[j - 1], vec=to)
+
+    def from_lane(j):
+        block = lax.rem(lane + NB - j, NB)
+        return (
+            send(held.at[:, :, rows_of(block), :], held.at[:, :, rows_of(block), :], vec_send.at[j - 1], vec_recv.at[j - 1], vec=block),
+            send(edges.at[0], edge.at[block], edge_send.at[j - 1], edge_recv.at[j - 1], vec=block),
+        )
+
+    for n in range(1, WINDOW + 1):
+        piece(step_of(n)).start()
+
     place = lax.broadcasted_iota(jnp.int32, (16, CHUNK), 1)
+    row = lax.broadcasted_iota(jnp.int32, (NV, NV), 0)
+    col = lax.broadcasted_iota(jnp.int32, (NV, NV), 1)
+    source = (row % NB) * VB + (row // NB % (NX * NH)) * NY + row // (NB * NX * NH)
+    order[...] = (col == source).astype(jnp.float32).astype(jnp.bfloat16)
+
+    def in_order(rows):
+        return jnp.dot(order[...], rows, preferred_element_type=jnp.float32).astype(jnp.bfloat16)
+
     own_in.wait()
 
     def pack(i, carry):
@@ -162,38 +207,10 @@
     mine_in.wait()
     links_in.wait()
 
-    pl.semaphore_wait(barrier, NH * NB - 1 + NX * NY - 1 + 2 + relays.astype(jnp.int32))
-
-    def piece(j):
-        to = lax.rem(lane + j, NB)
-        return send(
-            vec_hbm.at[0, :, :, :, lanes_of(flip(z_hi, to))],
-            held.at[:, :, rows_of(lane), :],
-            vec_send.at[j - 1],
-            vec_recv.at[j - 1],
-            vec=to,
-        )
-
-    def edge_piece(j):
-        to = lax.rem(lane + j, NB)
-        return send(edges.at[flip(z_hi, to)], edge.at[lane], edge_send.at[j - 1], edge_recv.at[j - 1], vec=to)
-
-    def from_lane(j):
-        block = lax.rem(lane + NB - j, NB)
-        return (
-            send(held.at[:, :, rows_of(block), :], held.at[:, :, rows_of(block), :], vec_send.at[j - 1], vec_recv.at[j - 1], vec=block),
-            send(edges.at[0], edge.at[block], edge_send.at[j - 1], edge_recv.at[j - 1], vec=block),
-        )
-
-    def start_pieces(j, carry):
-        piece(j).start()
-        return carry
-
-    def start_edges(j, carry):
-        edge_piece(j).start()
-        return carry
-
-    lax.fori_loop(1, NB, start_pieces, 0)
+    def start_edges(n, carry):
+        edge_piece(step_of(n)).start()
+        return carry
+
     lax.fori_loop(1, NB, start_edges, 0)
 
     def halo(block):
@@ -207,33 +224,33 @@
             device_id_type=pl.DeviceIdType.MESH,
         )
 
-    def to_relay(j, block):
-        n = lax.div(j, NY)
+    def to_relay(n, block):
+        slot = lax.div(n, NY)
         return send(
             held.at[:, :, rows_of(block), :],
-            hold.at[n],
+            hold.at[slot],
             halo_send.at[block],
-            hold_recv.at[n],
-            space=at(x, z_hi, lax.rem(j, NY), core),
-        )
-
-    def start_halo(j, block):
-        aside = jnp.logical_and(crossing, lax.rem(j, NY) != 0)
+            hold_recv.at[slot],
+            space=at(x, z_hi, lax.rem(n + 1, NY), core),
+        )
+
+    def start_halo(n, block):
+        aside = jnp.logical_and(crossing, lax.rem(n + 1, NY) != 0)
 
         @pl.when(aside)
         def _():
-            to_relay(j, block).start()
+            to_relay(n, block).start()
 
         @pl.when(jnp.logical_not(aside))
         def _():
             halo(block).start()
 
-    def handed(n):
-        block = lax.rem(lane + 2 * NB - y - n * NY, NB)
+    def handed(slot):
+        block = block_of(lane, y - 1 + slot * NY)
         return pltpu.make_async_remote_copy(
-            src_ref=hold.at[n],
+            src_ref=hold.at[slot],
             dst_ref=above.at[:, :, rows_of(block), :],
-            send_sem=hold_send.at[n],
+            send_sem=hold_send.at[slot],
             recv_sem=halo_recv.at[block],
             device_id={"space": beyond, "vec": beyond_lane},
             device_id_type=pl.DeviceIdType.MESH,
@@ -297,35 +314,45 @@
     start_halo(0, lane)
     move_yz(lane)
 
-    def arrive(j, carry):
-        block = lax.rem(lane + NB - j, NB)
-        for copy in from_lane(j):
+    def arrive(n, carry):
+        piece(step_of(n)).wait_send()
+
+        @pl.when(n + WINDOW < NB)
+        def _():
+            piece(step_of(n + WINDOW)).start()
+
+        for copy in from_lane(step_of(n)):
             copy.wait_recv()
-        start_halo(j, block)
+        block = block_of(lane, n)
+        start_halo(n, block)
         move_yz(block)
 
-        @pl.when(jnp.logical_and(jnp.logical_and(relays, j > 2), lax.rem(j + 2, NY) == y))
+        @pl.when(jnp.logical_and(jnp.logical_and(relays, n > 1), lax.rem(n + NY - 1, NY) == y))
         def _():
-            hand_on(lax.div(j - 2, NY))
+            hand_on(lax.div(n - 2, NY))
 
         return carry
 
     lax.fori_loop(1, NB, arrive, 0)
 
-    @pl.when(jnp.logical_and(relays, y > 1))
+    @pl.when(jnp.logical_and(relays, y == NY - 1))
     def _():
         hand_on(1)
 
 
-    def product(mu):
-        left = [
-            jnp.concatenate([moved[mu, c, p] for c in range(3)] + [held[c, p] for c in range(3)], axis=1)
-            for p in range(2)
-        ]
-        right = [
-            jnp.concatenate([held[c, p] for c in range(3)] + [moved[mu, c, p] for c in range(3)], axis=1)
-            for p in range(2)
-        ]
+    tile = (NV, 128)
+    row_a = lax.broadcasted_iota(jnp.int32, tile, 0) % NB
+    slot = lax.broadcasted_iota(jnp.int32, tile, 1) // VB
+    low_tile = (row_a - slot + NB) % NB < NB // 2
+
+    def spread(rows):
+        return rows.reshape(NY, NX, 16, 128)
+
+    def product(mu, which, b):
+        moved_mu = [jnp.concatenate([moved[mu, c, p] for c in range(3)], axis=1) for p in range(2)]
+        held_all = [jnp.concatenate([held[c, p] for c in range(3)], axis=1) for p in range(2)]
+        left = [jnp.concatenate([in_order(moved_mu[p]), ordered[p]], axis=1) for p in range(2)]
+        right = [jnp.concatenate([held_all[p], moved_mu[p]], axis=1) for p in range(2)]
 
         def dot(p, q):
             return lax.dot_general(
@@ -333,42 +360,15 @@
             )
 
         for t, total in enumerate((dot(0, 0) + dot(1, 1), dot(0, 1) - dot(1, 0))):
-            for n in range(2):
-                phi[mu, t, n] = total[:, n * 128 : (n + 1) * 128]
-
-    wide = lax.broadcasted_iota(jnp.int32, (8, 128), 1)
-
-    def turned(mu, t, a, yy):
-        turn = ((a + NB - 3) % NB) * VB
-        first, second = (phi[mu, t, (n + turn // 128) % 2, pl.ds(a * VB + yy, 8, stride=NY), :] for n in range(2))
-        stay = 128 - turn % 128
-        if stay < 128:
-            first, second = pltpu.roll(first, stay, 1), pltpu.roll(second, stay, 1)
-            first, second = jnp.where(wide < stay, first, second), jnp.where(wide < stay, second, first)
-        return first, second
-
-    def lay(which, t, yy, b, a, rows):
-        for xx in range(NX):
-            parts[which, t, yy, xx, b, pl.ds(a, NH, stride=NB), :] = rows[NH * xx : NH * (xx + 1)]
-
-    def lay_first():
-        for t in range(2):
-            for a in range(NB):
-                for yy in range(NY):
-                    for b in range(2):
-                        lay(0, t, yy, b, a, turned(b + 1, t, a, yy)[0])
-
-    def lay_second():
-        for t in range(2):
-            for a in range(NB):
-                for yy in range(NY):
-                    last = []
-                    for mu in range(3):
-                        first, second = turned(mu, t, a, yy)
-                        if mu == 0:
-                            lay(1, t, yy, 0, a, first)
-                        last.append(pltpu.roll(second, (mu * VB + VB) % 128, 1))
-                    lay(1, t, yy, 1, a, jnp.where(wide < VB, last[0], jnp.where(wide < 2 * VB, last[1], last[2])))
+            low, high = total[:, :128], total[:, 128:]
+            parts[which, t, :, :, b] = spread(jnp.where(low_tile, low, high))
+            rest = jnp.where(low_tile, high, low)
+            if mu == 1:
+                far[t] = pltpu.roll(rest, VB, 1)
+            elif mu == 2:
+                far[t] = jnp.where(slot == (row_a + 1) % 4, far[t], pltpu.roll(rest, 2 * VB, 1))
+            else:
+                parts[which, t, :, :, 1] = spread(jnp.where(slot == row_a % 4, rest, far[t]))
 
     def swap(which, i):
         yy = lax.rem(y + i, NY)
@@ -424,20 +424,20 @@
         for b in range(2):
             sum_xy[:, 2 * which + b, :] = totals[b]
 
-    product(1)
-    product(2)
-    lay_first()
+    for p in range(2):
+        ordered[p] = in_order(jnp.concatenate([held[c, p] for c in range(3)], axis=1))
+    product(1, 0, 0)
+    product(2, 0, 1)
     sum_cores(0)
 
-    def arrive_x(j, carry):
-        block = lax.rem(up_lane + NB - j, NB)
+    def arrive_x(n, carry):
+        block = block_of(up_lane, n)
         halo(block).wait_recv()
         move_x(block)
         return carry
 
     lax.fori_loop(0, NB, arrive_x, 0)
-    product(0)
-    lay_second()
+    product(0, 1, 0)
     sum_cores(1)
     sum_chips(0)
     sum_chips(1)
@@ -470,10 +470,10 @@
 
     half = VB // 2
     for t in range(2):
-        total = both[t]
+        total = pltpu.roll(both[t], (4 - lane % 4) % 4 * VB, 1)
         for mu in range(3):
             for k in range(NK):
-                row, first = ((mu + 2) % 3, (3 - k) * VB) if k < 4 else (3, mu * VB)
+                row, first = ((mu + 2) % 3, (4 - k) % 4 * VB) if k < 4 else (3, mu * VB)
                 low = total[row : row + 1, first : first + half]
                 high = total[row : row + 1, first + half : first + VB]
                 at_row = (mu * NK + k) * 2 + t
@@ -484,9 +484,8 @@
             rows = pl.ds((mu * NK + offsets[q]) * 2, 2)
             out[d, q, :, 0, :] = picked[rows, :half]
 
-    def drain(j, carry):
-        piece(j).wait_send()
-        edge_piece(j).wait_send()
+    def drain(n, carry):
+        edge_piece(n).wait_send()
         return carry
 
     def drain_halo(block, carry):
@@ -545,7 +544,9 @@
             pltpu.VMEM((NB, VB, CHUNK), bf16),
             pltpu.VMEM((3, 3, 3, 2, CHUNK), f32),
             pltpu.VMEM((3, 3, 2, NV, CHUNK), bf16),
-            pltpu.VMEM((3, 2, 2, NV, 128), f32),
+            pltpu.VMEM((NV, NV), bf16),
+            pltpu.VMEM((2, NV, 3 * CHUNK), bf16),
+            pltpu.VMEM((2, NV, 128), f32),
             pltpu.VMEM((2, 2, NY, NX, 2, 16, 128), f32),
             pltpu.VMEM((2, NY, NX, 2, 16, 128), f32),
             pltpu.VMEM((2, NX * NY - 1, 2, 16, 128), f32),

time: 74.9 us -> 70.7 us (0.944)
  Pallas kernels: 73.4 us -> 69.2 us
    pallas_call x1, Pallas kernels: 73.4 us -> 69.2 us  [body(): pl.pallas_call(functools.partial(kernel, scale=scale), out_shape=jax.Shap...]
where the time goes in v5:
time: 70.7 us; the launch traced here: 70.5 us
  Pallas kernels  69.2 us (98%)
  local copies, waits for them, and re-layouts  1.32 us (2%)
    pallas_call x1, Pallas kernels, body(): pl.pallas_call(functools.partial(kernel, scale=scale), out_shape=jax.Shap...  69.2 us

profile of v5, /device:TPU:1, one launch (start us, length us, event | category | flops | bytes accessed | tf_op | source)
XLA Modules:
  0.0 70.5 jit_solution(62761914706716785)
XLA Ops:
  0.0 69.2 %elementals.1 = f32[3,5,2,1,16]{4,3,2,1,0:T(1,128)} custom-call(bf16[1,3,2,32,1024]{4,3,2,1,0:T(8,128)(2,1)} %vec_hbm.1, f32[1,3,3,3,2,1024]{5,4,3,2,1,0:T(2,128)} %link_hbm.1, s32[3]{0:T(128)} %directions.1, s32[5]{0:T(128)} %offsets.1), custom_call_target="tpu_custom_call" | custom-call | tf_op jit(solution)/shard_map/elementals/pallas_call | solution.py:528
  69.2 1.3 %copy.6 = f32[3,5,2,1,16]{4,3,2,1,0:T(1,128)} copy(f32[3,5,2,1,16]{4,3,2,1,0:T(1,128)} %elementals.1) | data formatting | bytes 3840

commit v6 on v5

--- a/solution.py
+++ b/solution.py
@@ -13,7 +13,6 @@
 VB = 32
 NV = 256
 NB = NV // VB
-WINDOW = 7
 NK = 5
 CHUNK = SITES // NB
 NX, NH, NY, NC = 4, 2, 4, 2
@@ -53,7 +52,6 @@
     got_xy,
     sum_xy,
     got_z,
-    both,
     picked,
     local_sem,
     vec_send,
@@ -70,8 +68,6 @@
     xy_recv,
     z_send,
     z_recv,
-    last_send,
-    last_recv,
     *,
     scale,
 ):
@@ -125,29 +121,65 @@
             barrier, inc=1, device_id={"space": space, "vec": lane}, device_id_type=pl.DeviceIdType.MESH
         )
 
-    def greet_z(j, carry):
-        there, peer = z_peer(j)
-        greet(at(x, there, y, core), peer)
-        return carry
-
-    lax.fori_loop(0, NH * NB - 1, greet_z, 0)
-    for i in range(1, NX * NY):
-        greet(at(lax.rem(x + i % NX, NX), z_hi, lax.rem(y + i // NX, NY), core), lane)
-    greet(up, up_lane)
-    greet(down, down_lane)
-
     crossing = jnp.logical_and(y == 0, core == 0)
     crossed = jnp.logical_and(y == NY - 1, core == NC - 1)
     relays = jnp.logical_and(y > 0, core == 0)
     beyond = lax.rem(at(x, z_hi, 0, 0) + planes - 1, planes)
     beyond_lane = flip(half_of(beyond), chunk)
 
-    @pl.when(crossed)
-    def _():
-        for q in range(1, NY):
-            greet(up + q * NC, up_lane)
-
-    pl.semaphore_wait(barrier, NH * NB - 1 + NX * NY - 1 + 2 + relays.astype(jnp.int32))
+    lower_half = z_hi == 0
+
+    def greet_near(j, carry):
+        greet(space, lax.rem(lane + j, NB))
+        return carry
+
+    def greet_far():
+        def greet_z(j, carry):
+            greet(at(x, 1 - z_hi, y, core), j)
+            return carry
+
+        lax.fori_loop(0, NB, greet_z, 0)
+
+        @pl.when(crossing)
+        def _():
+            greet(down, down_lane)
+
+        @pl.when(crossed)
+        def _():
+            for q in range(NY):
+                greet(up + q * NC, up_lane)
+
+        @pl.when(relays)
+        def _():
+            greet(beyond, beyond_lane)
+
+    lax.fori_loop(1, NB, greet_near, 0)
+
+    @pl.when(jnp.logical_not(crossed))
+    def _():
+        greet(up, up_lane)
+
+    @pl.when(jnp.logical_not(crossing))
+    def _():
+        greet(down, down_lane)
+
+    for i in range(1, NX * NY):
+        greet(at(lax.rem(x + i % NX, NX), z_hi, lax.rem(y + i // NX, NY), core), lane)
+
+    def one(flag):
+        return flag.astype(jnp.int32)
+
+    near_count = NB - 1 + NX * NY - 1 + 2 - one(crossed) - one(crossing)
+    far_count = NB + one(crossing) + one(relays) + NY * one(crossed)
+
+    @pl.when(lower_half)
+    def _():
+        pl.semaphore_wait(barrier, near_count)
+        greet_far()
+
+    @pl.when(jnp.logical_not(lower_half))
+    def _():
+        pl.semaphore_wait(barrier, near_count + far_count)
 
     def step_of(n):
         if isinstance(n, int):
@@ -178,8 +210,12 @@
             send(edges.at[0], edge.at[block], edge_send.at[j - 1], edge_recv.at[j - 1], vec=block),
         )
 
-    for n in range(1, WINDOW + 1):
+    for n in range(1, NB):
         piece(step_of(n)).start()
+
+    @pl.when(jnp.logical_not(lower_half))
+    def _():
+        greet_far()
 
     place = lax.broadcasted_iota(jnp.int32, (16, CHUNK), 1)
     row = lax.broadcasted_iota(jnp.int32, (NV, NV), 0)
@@ -212,6 +248,10 @@
         return carry
 
     lax.fori_loop(1, NB, start_edges, 0)
+
+    @pl.when(lower_half)
+    def _():
+        pl.semaphore_wait(barrier, far_count)
 
     def halo(block):
         rows = rows_of(block)
@@ -315,12 +355,6 @@
     move_yz(lane)
 
     def arrive(n, carry):
-        piece(step_of(n)).wait_send()
-
-        @pl.when(n + WINDOW < NB)
-        def _():
-            piece(step_of(n + WINDOW)).start()
-
         for copy in from_lane(step_of(n)):
             copy.wait_recv()
         block = block_of(lane, n)
@@ -345,8 +379,15 @@
     slot = lax.broadcasted_iota(jnp.int32, tile, 1) // VB
     low_tile = (row_a - slot + NB) % NB < NB // 2
 
-    def spread(rows):
-        return rows.reshape(NY, NX, 16, 128)
+    first_half = lax.broadcasted_iota(jnp.int32, tile, 1) % VB < VB // 2
+
+    def lay(which, b, real, imag):
+        halves = (
+            jnp.where(first_half, real, pltpu.roll(imag, VB // 2, 1)),
+            jnp.where(first_half, pltpu.roll(real, 128 - VB // 2, 1), imag),
+        )
+        for h in range(NC):
+            parts[which, h, :, :, b] = halves[h].reshape(NY, NX, 16, 128)
 
     def product(mu, which, b):
         moved_mu = [jnp.concatenate([moved[mu, c, p] for c in range(3)], axis=1) for p in range(2)]
@@ -359,16 +400,20 @@
                 left[p], right[q], (((1,), (1,)), ((), ())), preferred_element_type=jnp.float32
             )
 
+        near = []
         for t, total in enumerate((dot(0, 0) + dot(1, 1), dot(0, 1) - dot(1, 0))):
             low, high = total[:, :128], total[:, 128:]
-            parts[which, t, :, :, b] = spread(jnp.where(low_tile, low, high))
+            near.append(jnp.where(low_tile, low, high))
             rest = jnp.where(low_tile, high, low)
             if mu == 1:
                 far[t] = pltpu.roll(rest, VB, 1)
             elif mu == 2:
                 far[t] = jnp.where(slot == (row_a + 1) % 4, far[t], pltpu.roll(rest, 2 * VB, 1))
             else:
-                parts[which, t, :, :, 1] = spread(jnp.where(slot == row_a % 4, rest, far[t]))
+                far[t] = jnp.where(slot == row_a % 4, rest, far[t])
+        lay(which, b, near[0], near[1])
+        if mu == 0:
+            lay(which, 1, far[0], far[1])
 
     def swap(which, i):
         yy = lax.rem(y + i, NY)
@@ -462,61 +507,58 @@
         return total + got_z[j]
 
     lax.fori_loop(0, NH * NB - 1, z_start, 0)
-    both[core] = lax.fori_loop(0, NH * NB - 1, z_add, sum_xy[z_hi * NB + lane]) * scale
-    last = send(both.at[core], both.at[core], last_send, last_recv, space=sibling)
-    last.start()
-    last_in = send(both.at[1 - core], both.at[1 - core], last_send, last_recv, space=sibling)
-    last_in.wait_recv()
+
+    def drain(n, carry):
+        piece(n).wait_send()
+        edge_piece(n).wait_send()
+        return carry
+
+    def drain_halo(block, carry):
+        halo(block).wait_send()
+        return carry
+
+    @pl.when(relays)
+    def _():
+        for n in range(2):
+            handed(n).wait_send()
+
+    lax.fori_loop(1, NB, drain, 0)
+    lax.fori_loop(0, NB, drain_halo, 0)
+    for which in range(2):
+
+        def drain_swap(i, carry):
+            swap(which, i).wait_send()
+            return carry
+
+        def drain_xy(slot, carry):
+            to_xy(which, lax.div(slot + 1, NX), lax.rem(slot + 1, NX)).wait_send()
+            return carry
+
+        lax.fori_loop(1, NY + 1, drain_swap, 0)
+        lax.fori_loop(0, NX * NY - 1, drain_xy, 0)
+
+    total = lax.fori_loop(0, NH * NB - 1, z_add, sum_xy[z_hi * NB + lane]) * scale
+    total = pltpu.roll(total, (4 - lane % 4) % 4 * VB, 1)
 
     half = VB // 2
     for t in range(2):
-        total = pltpu.roll(both[t], (4 - lane % 4) % 4 * VB, 1)
         for mu in range(3):
             for k in range(NK):
-                row, first = ((mu + 2) % 3, (4 - k) % 4 * VB) if k < 4 else (3, mu * VB)
-                low = total[row : row + 1, first : first + half]
-                high = total[row : row + 1, first + half : first + VB]
+                row, slot_k = ((mu + 2) % 3, (4 - k) % 4) if k < 4 else (3, mu)
+                first = slot_k * VB + t * half
                 at_row = (mu * NK + k) * 2 + t
-                picked[at_row : at_row + 1, :half] = jnp.where(core == 0, low, high)
+                picked[at_row : at_row + 1, :half] = total[row : row + 1, first : first + half]
     for d in range(3):
         mu = directions[d]
         for q in range(NK):
             rows = pl.ds((mu * NK + offsets[q]) * 2, 2)
             out[d, q, :, 0, :] = picked[rows, :half]
 
-    def drain(n, carry):
-        edge_piece(n).wait_send()
-        return carry
-
-    def drain_halo(block, carry):
-        halo(block).wait_send()
-        return carry
-
-    @pl.when(relays)
-    def _():
-        for n in range(2):
-            handed(n).wait_send()
-
     def drain_z(j, carry):
         to_z(j).wait_send()
         return carry
 
-    lax.fori_loop(1, NB, drain, 0)
-    lax.fori_loop(0, NB, drain_halo, 0)
-    for which in range(2):
-
-        def drain_swap(i, carry):
-            swap(which, i).wait_send()
-            return carry
-
-        def drain_xy(slot, carry):
-            to_xy(which, lax.div(slot + 1, NX), lax.rem(slot + 1, NX)).wait_send()
-            return carry
-
-        lax.fori_loop(1, NY + 1, drain_swap, 0)
-        lax.fori_loop(0, NX * NY - 1, drain_xy, 0)
     lax.fori_loop(0, NH * NB - 1, drain_z, 0)
-    last.wait_send()
 
 
 def body(vectors, links, directions, offsets):
@@ -552,7 +594,6 @@
             pltpu.VMEM((2, NX * NY - 1, 2, 16, 128), f32),
             pltpu.VMEM((16, 4, 128), f32),
             pltpu.VMEM((zs, 4, 128), f32),
-            pltpu.VMEM((2, 4, 128), f32),
             pltpu.VMEM((6 * NK + 2, 128), f32),
             dma((3,)),
             dma((NB - 1,)),
@@ -569,8 +610,6 @@
             dma((2, NX * NY - 1)),
             dma((zs,)),
             dma((zs,)),
-            dma,
-            dma,
         ],
         compiler_params=pltpu.CompilerParams(
             collective_id=0, has_side_effects=True, vmem_limit_bytes=63 * 1024 * 1024

time: 70.7 us -> 67.4 us (0.953); the launches traced: 70.5 us -> 66.2 us
  Pallas kernels: 69.2 us -> 64.9 us
    pallas_call x1, Pallas kernels: 69.2 us -> 64.9 us  [body(): pl.pallas_call(functools.partial(kernel, scale=scale), out_shape=jax.Shap...]
where the time goes in v6:
time: 67.4 us; the launch traced here: 66.2 us
  Pallas kernels  64.9 us (96%)
  local copies, waits for them, and re-layouts  1.32 us (2%)
    pallas_call x1, Pallas kernels, body(): pl.pallas_call(functools.partial(kernel, scale=scale), out_shape=jax.Shap...  64.9 us

profile of v6, /device:TPU:1, one launch (start us, length us, event | category | flops | bytes accessed | tf_op | source)
XLA Modules:
  0.0 66.2 jit_solution(13760873874895458389)
XLA Ops:
  0.0 64.9 %elementals.1 = f32[3,5,2,1,16]{4,3,2,1,0:T(1,128)} custom-call(bf16[1,3,2,32,1024]{4,3,2,1,0:T(8,128)(2,1)} %vec_hbm.1, f32[1,3,3,3,2,1024]{5,4,3,2,1,0:T(2,128)} %link_hbm.1, s32[3]{0:T(128)} %directions.1, s32[5]{0:T(128)} %offsets.1), custom_call_target="tpu_custom_call" | custom-call | tf_op jit(solution)/shard_map/elementals/pallas_call | solution.py:570
  64.9 1.3 %copy.6 = f32[3,5,2,1,16]{4,3,2,1,0:T(1,128)} copy(f32[3,5,2,1,16]{4,3,2,1,0:T(1,128)} %elementals.1) | data formatting | bytes 3840

commit v7 on v6

--- a/solution.py
+++ b/solution.py
@@ -54,6 +54,7 @@
     got_z,
     picked,
     local_sem,
+    own_sem,
     vec_send,
     vec_recv,
     edge_send,
@@ -98,15 +99,16 @@
     def lanes_of(chunk):
         return pl.ds(pl.multiple_of(chunk * CHUNK, CHUNK), CHUNK)
 
-    def rows_of(block):
-        return pl.ds(pl.multiple_of(block * VB, VB), VB)
-
-    own_in = pltpu.make_async_copy(vec_hbm.at[0], own, local_sem.at[0])
+    own_in = [
+        pltpu.make_async_copy(vec_hbm.at[0, :, :, :, pl.ds(c * CHUNK, CHUNK)], own.at[c], own_sem.at[c])
+        for c in range(NB)
+    ]
     links_in = pltpu.make_async_copy(link_hbm.at[0, :, :, :, :, lanes_of(chunk)], links, local_sem.at[1])
     mine_in = pltpu.make_async_copy(
-        vec_hbm.at[0, :, :, :, lanes_of(chunk)], held.at[:, :, rows_of(lane), :], local_sem.at[2]
+        vec_hbm.at[0, :, :, :, lanes_of(chunk)], held.at[lane], local_sem.at[0]
     )
-    own_in.start()
+    for copy in own_in:
+        copy.start()
     links_in.start()
     mine_in.start()
 
@@ -172,50 +174,8 @@
     near_count = NB - 1 + NX * NY - 1 + 2 - one(crossed) - one(crossing)
     far_count = NB + one(crossing) + one(relays) + NY * one(crossed)
 
-    @pl.when(lower_half)
-    def _():
-        pl.semaphore_wait(barrier, near_count)
-        greet_far()
-
-    @pl.when(jnp.logical_not(lower_half))
-    def _():
-        pl.semaphore_wait(barrier, near_count + far_count)
-
-    def step_of(n):
-        if isinstance(n, int):
-            return (NB // 2 + (2 * (n % 2) - 1) * (n // 2)) if n else 0
-        return (n > 0).astype(jnp.int32) * (NB // 2 + (2 * lax.rem(n, 2) - 1) * lax.div(n, 2))
-
-    def block_of(lane, n):
-        return lax.rem(lane + NB - step_of(n), NB)
-
-    def piece(j):
-        to = lax.rem(lane + j, NB)
-        return send(
-            vec_hbm.at[0, :, :, :, lanes_of(flip(z_hi, to))],
-            held.at[:, :, rows_of(lane), :],
-            vec_send.at[j - 1],
-            vec_recv.at[j - 1],
-            vec=to,
-        )
-
-    def edge_piece(j):
-        to = lax.rem(lane + j, NB)
-        return send(edges.at[flip(z_hi, to)], edge.at[lane], edge_send.at[j - 1], edge_recv.at[j - 1], vec=to)
-
-    def from_lane(j):
-        block = lax.rem(lane + NB - j, NB)
-        return (
-            send(held.at[:, :, rows_of(block), :], held.at[:, :, rows_of(block), :], vec_send.at[j - 1], vec_recv.at[j - 1], vec=block),
-            send(edges.at[0], edge.at[block], edge_send.at[j - 1], edge_recv.at[j - 1], vec=block),
-        )
-
-    for n in range(1, NB):
-        piece(step_of(n)).start()
-
-    @pl.when(jnp.logical_not(lower_half))
-    def _():
-        greet_far()
+    for copy in own_in:
+        copy.wait()
 
     place = lax.broadcasted_iota(jnp.int32, (16, CHUNK), 1)
     row = lax.broadcasted_iota(jnp.int32, (NV, NV), 0)
@@ -226,19 +186,63 @@
     def in_order(rows):
         return jnp.dot(order[...], rows, preferred_element_type=jnp.float32).astype(jnp.bfloat16)
 
-    own_in.wait()
 
     def pack(i, carry):
         to = lax.div(i, 2)
         rows = pl.ds(pl.multiple_of(lax.rem(i, 2) * 16, 16), 16)
         found = jnp.zeros((16, CHUNK), jnp.float32)
         for n in range(6):
-            field = own[n // 2, n % 2, rows, lanes_of(lax.rem(to + 1, NB))].astype(jnp.float32)
+            field = own[lax.rem(to + 1, NB), n // 2, n % 2, rows, :].astype(jnp.float32)
             found = jnp.where(place // LZ == n, pltpu.roll(field, n * LZ, 1) if n else field, found)
         edges[to, rows, :] = found.astype(jnp.bfloat16)
         return carry
 
     lax.fori_loop(0, 2 * NB, pack, 0)
+    @pl.when(lower_half)
+    def _():
+        pl.semaphore_wait(barrier, near_count)
+        greet_far()
+
+    @pl.when(jnp.logical_not(lower_half))
+    def _():
+        pl.semaphore_wait(barrier, near_count + far_count)
+
+    def step_of(n):
+        if isinstance(n, int):
+            return (NB // 2 + (2 * (n % 2) - 1) * (n // 2)) if n else 0
+        return (n > 0).astype(jnp.int32) * (NB // 2 + (2 * lax.rem(n, 2) - 1) * lax.div(n, 2))
+
+    def block_of(lane, n):
+        return lax.rem(lane + NB - step_of(n), NB)
+
+    def piece(j):
+        to = lax.rem(lane + j, NB)
+        return send(
+            own.at[flip(z_hi, to)],
+            held.at[lane],
+            vec_send.at[j - 1],
+            vec_recv.at[j - 1],
+            vec=to,
+        )
+
+    def edge_piece(j):
+        to = lax.rem(lane + j, NB)
+        return send(edges.at[flip(z_hi, to)], edge.at[lane], edge_send.at[j - 1], edge_recv.at[j - 1], vec=to)
+
+    def from_lane(j):
+        block = lax.rem(lane + NB - j, NB)
+        return (
+            send(held.at[block], held.at[block], vec_send.at[j - 1], vec_recv.at[j - 1], vec=block),
+            send(edges.at[0], edge.at[block], edge_send.at[j - 1], edge_recv.at[j - 1], vec=block),
+        )
+
+    for n in range(1, NB):
+        piece(step_of(n)).start()
+
+    @pl.when(jnp.logical_not(lower_half))
+    def _():
+        greet_far()
+
     edge[lane] = edges[chunk]
     mine_in.wait()
     links_in.wait()
@@ -254,10 +258,9 @@
         pl.semaphore_wait(barrier, far_count)
 
     def halo(block):
-        rows = rows_of(block)
         return pltpu.make_async_remote_copy(
-            src_ref=held.at[:, :, rows, :],
-            dst_ref=above.at[:, :, rows, :],
+            src_ref=held.at[block],
+            dst_ref=above.at[block],
             send_sem=halo_send.at[block],
             recv_sem=halo_recv.at[block],
             device_id={"space": down, "vec": down_lane},
@@ -267,7 +270,7 @@
     def to_relay(n, block):
         slot = lax.div(n, NY)
         return send(
-            held.at[:, :, rows_of(block), :],
+            held.at[block],
             hold.at[slot],
             halo_send.at[block],
             hold_recv.at[slot],
@@ -289,7 +292,7 @@
         block = block_of(lane, y - 1 + slot * NY)
         return pltpu.make_async_remote_copy(
             src_ref=hold.at[slot],
-            dst_ref=above.at[:, :, rows_of(block), :],
+            dst_ref=above.at[block],
             send_sem=hold_send.at[slot],
             recv_sem=halo_recv.at[block],
             device_id={"space": beyond, "vec": beyond_lane},
@@ -317,7 +320,7 @@
         def step(i, carry):
             first = pl.multiple_of(i * 16, 16)
             rows = pl.ds(pl.multiple_of(block * VB + first, 16), 16)
-            vecs = [[held[c, p, rows, :].astype(jnp.float32) for p in range(2)] for c in range(3)]
+            vecs = [[held[block, c, p, pl.ds(first, 16), :].astype(jnp.float32) for p in range(2)] for c in range(3)]
             border = edge[block, pl.ds(first, 16), :].astype(jnp.float32)
             along_y = [
                 [
@@ -346,20 +349,17 @@
     def move_x(block):
         def step(i, carry):
             rows = pl.ds(pl.multiple_of(block * VB + i * 16, 16), 16)
-            forward(0, rows, [[above[c, p, rows, :].astype(jnp.float32) for p in range(2)] for c in range(3)])
+            half = pl.ds(pl.multiple_of(i * 16, 16), 16)
+            forward(0, rows, [[above[block, c, p, half, :].astype(jnp.float32) for p in range(2)] for c in range(3)])
             return carry
 
         lax.fori_loop(0, 2, step, 0)
 
     start_halo(0, lane)
-    move_yz(lane)
 
     def arrive(n, carry):
-        for copy in from_lane(step_of(n)):
-            copy.wait_recv()
-        block = block_of(lane, n)
-        start_halo(n, block)
-        move_yz(block)
+        from_lane(step_of(n))[0].wait_recv()
+        start_halo(n, block_of(lane, n))
 
         @pl.when(jnp.logical_and(jnp.logical_and(relays, n > 1), lax.rem(n + NY - 1, NY) == y))
         def _():
@@ -372,6 +372,14 @@
     @pl.when(jnp.logical_and(relays, y == NY - 1))
     def _():
         hand_on(1)
+
+    def move(n, carry):
+        from_lane(step_of(n))[1].wait_recv()
+        move_yz(block_of(lane, n))
+        return carry
+
+    move_yz(lane)
+    lax.fori_loop(1, NB, move, 0)
 
 
     tile = (NV, 128)
@@ -391,7 +399,7 @@
 
     def product(mu, which, b):
         moved_mu = [jnp.concatenate([moved[mu, c, p] for c in range(3)], axis=1) for p in range(2)]
-        held_all = [jnp.concatenate([held[c, p] for c in range(3)], axis=1) for p in range(2)]
+        held_all = [jnp.concatenate([held[:, c, p].reshape(NV, CHUNK) for c in range(3)], axis=1) for p in range(2)]
         left = [jnp.concatenate([in_order(moved_mu[p]), ordered[p]], axis=1) for p in range(2)]
         right = [jnp.concatenate([held_all[p], moved_mu[p]], axis=1) for p in range(2)]
 
@@ -470,7 +478,7 @@
             sum_xy[:, 2 * which + b, :] = totals[b]
 
     for p in range(2):
-        ordered[p] = in_order(jnp.concatenate([held[c, p] for c in range(3)], axis=1))
+        ordered[p] = in_order(jnp.concatenate([held[:, c, p].reshape(NV, CHUNK) for c in range(3)], axis=1))
     product(1, 0, 0)
     product(2, 0, 1)
     sum_cores(0)
@@ -578,9 +586,9 @@
         ],
         out_specs=pl.BlockSpec(memory_space=pltpu.VMEM),
         scratch_shapes=[
-            pltpu.VMEM((3, 2, VB, SITES), bf16),
-            pltpu.VMEM((3, 2, NV, CHUNK), bf16),
-            pltpu.VMEM((3, 2, NV, CHUNK), bf16),
+            pltpu.VMEM((NB, 3, 2, VB, CHUNK), bf16),
+            pltpu.VMEM((NB, 3, 2, VB, CHUNK), bf16),
+            pltpu.VMEM((NB, 3, 2, VB, CHUNK), bf16),
             pltpu.VMEM((2, 3, 2, VB, CHUNK), bf16),
             pltpu.VMEM((NB, VB, CHUNK), bf16),
             pltpu.VMEM((NB, VB, CHUNK), bf16),
@@ -595,7 +603,8 @@
             pltpu.VMEM((16, 4, 128), f32),
             pltpu.VMEM((zs, 4, 128), f32),
             pltpu.VMEM((6 * NK + 2, 128), f32),
-            dma((3,)),
+            dma((2,)),
+            dma((NB,)),
             dma((NB - 1,)),
             dma((NB - 1,)),
             dma((NB - 1,)),

time: 67.4 us -> 65.6 us (0.973); the launches traced: 66.2 us -> 65.4 us
  Pallas kernels: 64.9 us -> 64.1 us
    pallas_call x1, Pallas kernels: 64.9 us -> 64.1 us  [body(): pl.pallas_call(functools.partial(kernel, scale=scale), out_shape=jax.Shap...]
where the time goes in v7:
time: 65.6 us; the launch traced here: 65.4 us
  Pallas kernels  64.1 us (98%)
  local copies, waits for them, and re-layouts  1.32 us (2%)
    pallas_call x1, Pallas kernels, body(): pl.pallas_call(functools.partial(kernel, scale=scale), out_shape=jax.Shap...  64.1 us
    unnamed x1, local copies, waits for them, and re-layouts  1.32 us

profile of v7, /device:TPU:1, one launch (start us, length us, event | category | flops | bytes accessed | tf_op | source)
XLA Modules:
  0.0 65.4 jit_solution(16992629022318245614)
XLA Ops:
  0.0 64.1 %elementals.1 = f32[3,5,2,1,16]{4,3,2,1,0:T(1,128)} custom-call(bf16[1,3,2,32,1024]{4,3,2,1,0:T(8,128)(2,1)} %vec_hbm.1, f32[1,3,3,3,2,1024]{5,4,3,2,1,0:T(2,128)} %link_hbm.1, s32[3]{0:T(128)} %directions.1, s32[5]{0:T(128)} %offsets.1), custom_call_target="tpu_custom_call" | custom-call | tf_op jit(solution)/shard_map/elementals/pallas_call | solution.py:578
  64.1 1.3 %copy.6 = f32[3,5,2,1,16]{4,3,2,1,0:T(1,128)} copy(f32[3,5,2,1,16]{4,3,2,1,0:T(1,128)} %elementals.1) | data formatting | bytes 3840

commit v8 on v7

--- a/solution.py
+++ b/solution.py
@@ -107,10 +107,6 @@
     mine_in = pltpu.make_async_copy(
         vec_hbm.at[0, :, :, :, lanes_of(chunk)], held.at[lane], local_sem.at[0]
     )
-    for copy in own_in:
-        copy.start()
-    links_in.start()
-    mine_in.start()
 
     def z_peer(j):
         near = (j >= NB).astype(jnp.int32)
@@ -167,6 +163,11 @@
 
     for i in range(1, NX * NY):
         greet(at(lax.rem(x + i % NX, NX), z_hi, lax.rem(y + i // NX, NY), core), lane)
+
+    for copy in own_in:
+        copy.start()
+    links_in.start()
+    mine_in.start()
 
     def one(flag):
         return flag.astype(jnp.int32)
@@ -236,8 +237,12 @@
             send(edges.at[0], edge.at[block], edge_send.at[j - 1], edge_recv.at[j - 1], vec=block),
         )
 
+    yields = jnp.logical_and(y == 0, core == NC - 1)
     for n in range(1, NB):
-        piece(step_of(n)).start()
+
+        @pl.when(jnp.logical_or(jnp.logical_not(yields), n <= 5))
+        def _():
+            piece(step_of(n)).start()
 
     @pl.when(jnp.logical_not(lower_half))
     def _():
@@ -367,6 +372,13 @@
 
         return carry
 
+    @pl.when(yields)
+    def _():
+        for n in range(1, 6):
+            piece(step_of(n)).wait_send()
+        for n in range(6, NB):
+            piece(step_of(n)).start()
+
     lax.fori_loop(1, NB, arrive, 0)
 
     @pl.when(jnp.logical_and(relays, y == NY - 1))
@@ -517,7 +529,10 @@
     lax.fori_loop(0, NH * NB - 1, z_start, 0)
 
     def drain(n, carry):
-        piece(n).wait_send()
+        @pl.when(jnp.logical_or(jnp.logical_not(yields), n > 5))
+        def _():
+            piece(step_of(n)).wait_send()
+
         edge_piece(n).wait_send()
         return carry
 

time: 65.6 us -> 65.6 us (level)
  no operation moved by 1% of the time
where the time goes in v8:
time: 65.6 us; the launch traced here: 65.3 us
  Pallas kernels  64 us (98%)
  local copies, waits for them, and re-layouts  1.32 us (2%)
    pallas_call x1, Pallas kernels, body(): pl.pallas_call(functools.partial(kernel, scale=scale), out_shape=jax.Shap...  64 us
    unnamed x1, local copies, waits for them, and re-layouts  1.32 us

profile of v8, /device:TPU:1, one launch (start us, length us, event | category | flops | bytes accessed | tf_op | source)
XLA Modules:
  0.0 65.3 jit_solution(4045583791411865066)
XLA Ops:
  0.0 64.0 %elementals.1 = f32[3,5,2,1,16]{4,3,2,1,0:T(1,128)} custom-call(bf16[1,3,2,32,1024]{4,3,2,1,0:T(8,128)(2,1)} %vec_hbm.1, f32[1,3,3,3,2,1024]{5,4,3,2,1,0:T(2,128)} %link_hbm.1, s32[3]{0:T(128)} %directions.1, s32[5]{0:T(128)} %offsets.1), custom_call_target="tpu_custom_call" | custom-call | tf_op jit(solution)/shard_map/elementals/pallas_call | solution.py:593
  64.0 1.3 %copy.6 = f32[3,5,2,1,16]{4,3,2,1,0:T(1,128)} copy(f32[3,5,2,1,16]{4,3,2,1,0:T(1,128)} %elementals.1) | data formatting | bytes 3840

commit v9 on v8

--- a/solution.py
+++ b/solution.py
@@ -420,8 +420,16 @@
                 left[p], right[q], (((1,), (1,)), ((), ())), preferred_element_type=jnp.float32
             )
 
+        def both_parts():
+            return lax.dot_general(
+                jnp.concatenate(left, axis=1),
+                jnp.concatenate(right, axis=1),
+                (((1,), (1,)), ((), ())),
+                preferred_element_type=jnp.float32,
+            )
+
         near = []
-        for t, total in enumerate((dot(0, 0) + dot(1, 1), dot(0, 1) - dot(1, 0))):
+        for t, total in enumerate((both_parts(), dot(0, 1) - dot(1, 0))):
             low, high = total[:, :128], total[:, 128:]
             near.append(jnp.where(low_tile, low, high))
             rest = jnp.where(low_tile, high, low)
@@ -435,6 +443,9 @@
         if mu == 0:
             lay(which, 1, far[0], far[1])
 
+    def line(i):
+        return i + (i == 1).astype(jnp.int32) - (i == 2).astype(jnp.int32)
+
     def swap(which, i):
         yy = lax.rem(y + i, NY)
         return send(
@@ -458,7 +469,7 @@
 
     def sum_cores(which):
         def swap_start(i, carry):
-            swap(which, i).start()
+            swap(which, line(i)).start()
             return carry
 
         def swap_add(i):
@@ -467,9 +478,10 @@
             parts[which, core, yy] = parts[which, core, yy] + swapped[which, yy]
 
         def xy_start(i, carry):
-            swap_add(i)
-            for j in range(NX):
-                to_xy(which, i, j).start()
+            far_i = line(i)
+            swap_add(far_i)
+            for j in (2, 1, 3, 0):
+                to_xy(which, far_i, j).start()
             return carry
 
         lax.fori_loop(1, NY + 1, swap_start, 0)

time: 65.6 us -> 65.2 us (level)
  no operation moved by 1% of the time
where the time goes in v9:
time: 65.2 us; the launch traced here: 64.9 us
  Pallas kernels  63.5 us (97%)
  local copies, waits for them, and re-layouts  1.32 us (2%)
    pallas_call x1, Pallas kernels, body(): pl.pallas_call(functools.partial(kernel, scale=scale), out_shape=jax.Shap...  63.5 us
    unnamed x1, local copies, waits for them, and re-layouts  1.32 us

profile of v9, /device:TPU:1, one launch (start us, length us, event | category | flops | bytes accessed | tf_op | source)
XLA Modules:
  0.0 64.9 jit_solution(2087012391220853350)
XLA Ops:
  0.0 63.5 %elementals.1 = f32[3,5,2,1,16]{4,3,2,1,0:T(1,128)} custom-call(bf16[1,3,2,32,1024]{4,3,2,1,0:T(8,128)(2,1)} %vec_hbm.1, f32[1,3,3,3,2,1024]{5,4,3,2,1,0:T(2,128)} %link_hbm.1, s32[3]{0:T(128)} %directions.1, s32[5]{0:T(128)} %offsets.1), custom_call_target="tpu_custom_call" | custom-call | tf_op jit(solution)/shard_map/elementals/pallas_call | solution.py:605
  63.6 1.3 %copy.6 = f32[3,5,2,1,16]{4,3,2,1,0:T(1,128)} copy(f32[3,5,2,1,16]{4,3,2,1,0:T(1,128)} %elementals.1) | data formatting | bytes 3840

commit v10 on v9

--- a/solution.py
+++ b/solution.py
@@ -538,7 +538,7 @@
         to_z(j).wait_recv()
         return total + got_z[j]
 
-    lax.fori_loop(0, NH * NB - 1, z_start, 0)
+    lax.fori_loop(0, NH * NB - 1, z_start, 0, unroll=True)
 
     def drain(n, carry):
         @pl.when(jnp.logical_or(jnp.logical_not(yields), n > 5))
@@ -572,7 +572,7 @@
         lax.fori_loop(1, NY + 1, drain_swap, 0)
         lax.fori_loop(0, NX * NY - 1, drain_xy, 0)
 
-    total = lax.fori_loop(0, NH * NB - 1, z_add, sum_xy[z_hi * NB + lane]) * scale
+    total = lax.fori_loop(0, NH * NB - 1, z_add, sum_xy[z_hi * NB + lane], unroll=True) * scale
     total = pltpu.roll(total, (4 - lane % 4) % 4 * VB, 1)
 
     half = VB // 2

time: 65.2 us -> 65.1 us (level)
  no operation moved by 1% of the time
where the time goes in v10:
time: 65.1 us; the launch traced here: 64.9 us
  Pallas kernels  63.6 us (98%)
  local copies, waits for them, and re-layouts  1.32 us (2%)
    pallas_call x1, Pallas kernels, body(): pl.pallas_call(functools.partial(kernel, scale=scale), out_shape=jax.Shap...  63.6 us
    unnamed x1, local copies, waits for them, and re-layouts  1.32 us

profile of v10, /device:TPU:1, one launch (start us, length us, event | category | flops | bytes accessed | tf_op | source)
XLA Modules:
  0.0 64.9 jit_solution(12058968979772813943)
XLA Ops:
  0.0 63.6 %elementals.1 = f32[3,5,2,1,16]{4,3,2,1,0:T(1,128)} custom-call(bf16[1,3,2,32,1024]{4,3,2,1,0:T(8,128)(2,1)} %vec_hbm.1, f32[1,3,3,3,2,1024]{5,4,3,2,1,0:T(2,128)} %link_hbm.1, s32[3]{0:T(128)} %directions.1, s32[5]{0:T(128)} %offsets.1), custom_call_target="tpu_custom_call" | custom-call | tf_op jit(solution)/shard_map/elementals/pallas_call | solution.py:605
  63.6 1.3 %copy.6 = f32[3,5,2,1,16]{4,3,2,1,0:T(1,128)} copy(f32[3,5,2,1,16]{4,3,2,1,0:T(1,128)} %elementals.1) | data formatting | bytes 3840
